TPU v7x, 128 devices: a whole 4x4x4 slice. The times are simulated.
128 devices in a mesh: blk: 16 (over x_hi, z, core), narrow: 8 (over y, x_lo).
Axes of the slice: x: 4 (x_hi: 2, x_lo: 2; x = x_hi * 2 + x_lo), y: 4, z: 4, core: 2. Of those that a mesh axis runs over, the one named last changes fastest.
Arguments:
- points: float32 [32, 65536], P(None, ('blk', 'narrow')), may hold values from -4.5 to 4.5
- lengthscale: float32 [32], replicated, may hold values from 2.5 to 5
- noise: float32 [1], replicated, may hold values from 0.3 to 1
- solution: float32 [17, 65536], P(None, ('blk', 'narrow')), may hold values from -6 to 6
- residual: float32 [17, 65536], P(None, ('blk', 'narrow')), may hold values from -6 to 6
- direction: float32 [17, 65536], P(None, ('blk', 'narrow')), may hold values from -6 to 6
Outputs:
- new_solution: float32 [17, 65536], P(None, ('blk', 'narrow'))
- new_residual: float32 [17, 65536], P(None, ('blk', 'narrow'))
- new_direction: float32 [17, 65536], P(None, ('blk', 'narrow'))
All inputs are finite; a program needn't handle non-finite values.
Results may differ from a plain program's by a relative error of at most 0.000086.
Values sent between devices are 32-bit elements; how exact they have to be, the bound alone decides.
A program may use at most 64 MiB of HBM per device.

v0:
```python
import math

import jax
import jax.numpy as jnp
from jax import lax
from jax.sharding import PartitionSpec as P


def from_behind(block, axis, distance):
    devices = range(lax.axis_size(axis))
    route = [((i - distance) % len(devices), i) for i in devices]
    return lax.ppermute(block, axis, route)


def matern(cross, sq_rows, sq_cols):
    squared = jnp.maximum(sq_rows[:, None] + sq_cols[None, :] - 2.0 * cross, 0.0)
    scaled_dist = jnp.sqrt(squared) * math.sqrt(5.0)
    return (1.0 + scaled_dist + scaled_dist * scaled_dist / 3.0) * jnp.exp(-scaled_dist)


def gram(left, right):
    return lax.dot_general(left, right, (((1,), (1,)), ((), ())), precision=lax.Precision.HIGHEST)


def on_device(points, lengthscale, noise, solution, residual, direction):
    hi = lax.Precision.HIGHEST
    scaled = points / lengthscale[:, None]
    feats = scaled.shape[0]
    sides = direction.shape[0]
    rows_dev = scaled.shape[1]
    cycle_size = lax.axis_size("blk")
    block_pts = lax.all_gather(scaled, "narrow", axis=1, tiled=True)
    width = block_pts.shape[1]
    sq_block = jnp.sum(block_pts * block_pts, 0)

    def visit(cols_pts, cols_dir):
        sq_cols = jnp.sum(cols_pts * cols_pts, 0)
        cross = lax.dot_general(block_pts, cols_pts, (((0,), (0,)), ((), ())), precision=hi)
        kern = matern(cross, sq_block, sq_cols)
        forward = gram(cols_dir, kern)
        return (forward, jnp.zeros((sides, rows_dev), jnp.float32))

    empty_acc = jnp.zeros((sides, width), jnp.float32)

    def cycle_step(index, carry):
        packet, acc = carry
        acc = acc + visit(packet[:feats], packet[feats:])[0]
        packet = from_behind(packet, "blk", 1)
        return (packet, acc)

    start = jnp.concatenate([scaled, direction], 0)
    packet, acc = lax.fori_loop(0, cycle_size - 1, cycle_step, (start, empty_acc))
    acc = acc + visit(packet[:feats], packet[feats:])[0]
    summed = lax.psum_scatter(acc, "narrow", scatter_dimension=1, tiled=True)
    image = summed + noise[0] * direction
    curvature, correlation = lax.psum(
        (gram(direction, image), gram(direction, residual)), ("blk", "narrow")
    )
    factor = jnp.linalg.cholesky(curvature)
    step_coef = jax.scipy.linalg.cho_solve((factor, True), correlation)
    new_residual = residual - jnp.dot(step_coef.T, image, precision=hi)
    update = lax.psum(gram(image, new_residual), ("blk", "narrow"))
    new_solution = solution + jnp.dot(step_coef.T, direction, precision=hi)
    conj_coef = -jax.scipy.linalg.cho_solve((factor, True), update)
    new_direction = new_residual + jnp.dot(conj_coef.T, direction, precision=hi)
    return (new_solution, new_residual, new_direction)


def solution(mesh):
    placed = (
        P(None, ("blk", "narrow")),
        P(),
        P(),
        P(None, ("blk", "narrow")),
        P(None, ("blk", "narrow")),
        P(None, ("blk", "narrow")),
    )
    return jax.shard_map(
        on_device,
        mesh=mesh,
        in_specs=placed,
        out_specs=(
            P(None, ("blk", "narrow")),
            P(None, ("blk", "narrow")),
            P(None, ("blk", "narrow")),
        ),
        check_vma=False,
    )
```

profile of v0, /device:TPU:1, one launch (start us, length us, event | category | flops | bytes accessed | tf_op | source)
XLA Modules:
  0.0 614.0 jit_solution(13394216698869581859)
XLA Ops:
  8.1 25.5 %all_gather.3 = f32[32,4096]{1,0:T(8,128)S(1)} all-gather(f32[32,512]{1,0:T(8,128)S(1)} %broadcast_divide_fusion), channel_id=1, replica_groups=mesh['blk'=16,'narrow'=8] {'narrow'}, dimensions={1}, use_global_device_ids=true | all-gather | bytes 589824 | tf_op jit(solution)/shard_map/all_gather | solution.py:32
  34.5 376.9 %while.13 = (s32[]{:T(128)}, f32[49,512]{1,0:T(8,128)S(1)}, f32[17,4096]{1,0:T(8,128)S(1)}, f32[4096]{0:T(1024)S(1)}, f32[32,4096]{1,0:T(8,128)S(1)}, /*index=5*/s32[]{:T(128)}, s32[]{:T(128)}) while((s32[]{:T(128)}, f32[49,512]{1,0:T(8,128)S(1)}, f32[17,4096]{1,0:T(8,128)S(1)}, f32[4096]{0:T(1024)S(1)}, f32[32,4096]{1,0:T(8,128)S(1)}, ...), condition=%wide.region_3.0_spmd.clone, body=%wide.region_1.0_spmd.clone.sunk | while | flops 1256365568 | bytes 18776192 | solution.py:52
  42.5 8.9 %fusion.103 = f32[4096,512]{1,0:T(8,128)} fusion(f32[32,4096]{1,0:T(8,128)S(1)} %get-tuple-element.113, f32[49,512]{1,0:T(8,128)S(1)} %copy.14), kind=kOutput, calls=%fused_computation.24.clone.1 | convolution fusion | flops 805306368 | bytes 8978432 | tf_op jit(solution)/shard_map/while/body/eval_jaxpr/dot_general | solution.py:38
  51.4 14.8 %fusion.104 = f32[17,4096]{1,0:T(8,128)S(1)} fusion(f32[4096,512]{1,0:T(8,128)} %fusion.103, f32[512]{0:T(512)S(1)} %multiply_reduce_fusion.4, f32[4096]{0:T(1024)S(1)} %get-tuple-element.112, f32[17,4096]{1,0:T(8,128)S(1)} %get-tuple-element.104, pred[]{:T(512)S(6)} %compare.15, f32[49,512]{1,0:T(8,128)S(1)} %copy.14), kind=kOutput, calls=%fused_computation.15.clone.1 | convolution fusion | flops 451026944 | bytes 9127937 | tf_op jit(solution)/shard_map/while/body/eval_jaxpr/dot_general | solution.py:22
  66.3 8.9 %fusion.103 = f32[4096,512]{1,0:T(8,128)} fusion(f32[32,4096]{1,0:T(8,128)S(1)} %get-tuple-element.113, f32[49,512]{1,0:T(8,128)S(1)} %copy.14), kind=kOutput, calls=%fused_computation.24.clone.1 | convolution fusion | flops 805306368 | bytes 8978432 | tf_op jit(solution)/shard_map/while/body/eval_jaxpr/dot_general | solution.py:38
  75.3 14.8 %fusion.104 = f32[17,4096]{1,0:T(8,128)S(1)} fusion(f32[4096,512]{1,0:T(8,128)} %fusion.103, f32[512]{0:T(512)S(1)} %multiply_reduce_fusion.4, f32[4096]{0:T(1024)S(1)} %get-tuple-element.112, f32[17,4096]{1,0:T(8,128)S(1)} %get-tuple-element.104, pred[]{:T(512)S(6)} %compare.15, f32[49,512]{1,0:T(8,128)S(1)} %copy.14), kind=kOutput, calls=%fused_computation.15.clone.1 | convolution fusion | flops 451026944 | bytes 9127937 | tf_op jit(solution)/shard_map/while/body/eval_jaxpr/dot_general | solution.py:22
  92.2 8.9 %fusion.103 = f32[4096,512]{1,0:T(8,128)} fusion(f32[32,4096]{1,0:T(8,128)S(1)} %get-tuple-element.113, f32[49,512]{1,0:T(8,128)S(1)} %copy.14), kind=kOutput, calls=%fused_computation.24.clone.1 | convolution fusion | flops 805306368 | bytes 8978432 | tf_op jit(solution)/shard_map/while/body/eval_jaxpr/dot_general | solution.py:38
  101.1 14.8 %fusion.104 = f32[17,4096]{1,0:T(8,128)S(1)} fusion(f32[4096,512]{1,0:T(8,128)} %fusion.103, f32[512]{0:T(512)S(1)} %multiply_reduce_fusion.4, f32[4096]{0:T(1024)S(1)} %get-tuple-element.112, f32[17,4096]{1,0:T(8,128)S(1)} %get-tuple-element.104, pred[]{:T(512)S(6)} %compare.15, f32[49,512]{1,0:T(8,128)S(1)} %copy.14), kind=kOutput, calls=%fused_computation.15.clone.1 | convolution fusion | flops 451026944 | bytes 9127937 | tf_op jit(solution)/shard_map/while/body/eval_jaxpr/dot_general | solution.py:22
  116.1 8.9 %fusion.103 = f32[4096,512]{1,0:T(8,128)} fusion(f32[32,4096]{1,0:T(8,128)S(1)} %get-tuple-element.113, f32[49,512]{1,0:T(8,128)S(1)} %copy.14), kind=kOutput, calls=%fused_computation.24.clone.1 | convolution fusion | flops 805306368 | bytes 8978432 | tf_op jit(solution)/shard_map/while/body/eval_jaxpr/dot_general | solution.py:38
  125.0 14.8 %fusion.104 = f32[17,4096]{1,0:T(8,128)S(1)} fusion(f32[4096,512]{1,0:T(8,128)} %fusion.103, f32[512]{0:T(512)S(1)} %multiply_reduce_fusion.4, f32[4096]{0:T(1024)S(1)} %get-tuple-element.112, f32[17,4096]{1,0:T(8,128)S(1)} %get-tuple-element.104, pred[]{:T(512)S(6)} %compare.15, f32[49,512]{1,0:T(8,128)S(1)} %copy.14), kind=kOutput, calls=%fused_computation.15.clone.1 | convolution fusion | flops 451026944 | bytes 9127937 | tf_op jit(solution)/shard_map/while/body/eval_jaxpr/dot_general | solution.py:22
  141.6 8.9 %fusion.103 = f32[4096,512]{1,0:T(8,128)} fusion(f32[32,4096]{1,0:T(8,128)S(1)} %get-tuple-element.113, f32[49,512]{1,0:T(8,128)S(1)} %copy.14), kind=kOutput, calls=%fused_computation.24.clone.1 | convolution fusion | flops 805306368 | bytes 8978432 | tf_op jit(solution)/shard_map/while/body/eval_jaxpr/dot_general | solution.py:38
  150.6 14.8 %fusion.104 = f32[17,4096]{1,0:T(8,128)S(1)} fusion(f32[4096,512]{1,0:T(8,128)} %fusion.103, f32[512]{0:T(512)S(1)} %multiply_reduce_fusion.4, f32[4096]{0:T(1024)S(1)} %get-tuple-element.112, f32[17,4096]{1,0:T(8,128)S(1)} %get-tuple-element.104, pred[]{:T(512)S(6)} %compare.15, f32[49,512]{1,0:T(8,128)S(1)} %copy.14), kind=kOutput, calls=%fused_computation.15.clone.1 | convolution fusion | flops 451026944 | bytes 9127937 | tf_op jit(solution)/shard_map/while/body/eval_jaxpr/dot_general | solution.py:22
  165.5 8.9 %fusion.103 = f32[4096,512]{1,0:T(8,128)} fusion(f32[32,4096]{1,0:T(8,128)S(1)} %get-tuple-element.113, f32[49,512]{1,0:T(8,128)S(1)} %copy.14), kind=kOutput, calls=%fused_computation.24.clone.1 | convolution fusion | flops 805306368 | bytes 8978432 | tf_op jit(solution)/shard_map/while/body/eval_jaxpr/dot_general | solution.py:38
  174.4 14.8 %fusion.104 = f32[17,4096]{1,0:T(8,128)S(1)} fusion(f32[4096,512]{1,0:T(8,128)} %fusion.103, f32[512]{0:T(512)S(1)} %multiply_reduce_fusion.4, f32[4096]{0:T(1024)S(1)} %get-tuple-element.112, f32[17,4096]{1,0:T(8,128)S(1)} %get-tuple-element.104, pred[]{:T(512)S(6)} %compare.15, f32[49,512]{1,0:T(8,128)S(1)} %copy.14), kind=kOutput, calls=%fused_computation.15.clone.1 | convolution fusion | flops 451026944 | bytes 9127937 | tf_op jit(solution)/shard_map/while/body/eval_jaxpr/dot_general | solution.py:22
  191.0 8.9 %fusion.103 = f32[4096,512]{1,0:T(8,128)} fusion(f32[32,4096]{1,0:T(8,128)S(1)} %get-tuple-element.113, f32[49,512]{1,0:T(8,128)S(1)} %copy.14), kind=kOutput, calls=%fused_computation.24.clone.1 | convolution fusion | flops 805306368 | bytes 8978432 | tf_op jit(solution)/shard_map/while/body/eval_jaxpr/dot_general | solution.py:38
  199.9 14.8 %fusion.104 = f32[17,4096]{1,0:T(8,128)S(1)} fusion(f32[4096,512]{1,0:T(8,128)} %fusion.103, f32[512]{0:T(512)S(1)} %multiply_reduce_fusion.4, f32[4096]{0:T(1024)S(1)} %get-tuple-element.112, f32[17,4096]{1,0:T(8,128)S(1)} %get-tuple-element.104, pred[]{:T(512)S(6)} %compare.15, f32[49,512]{1,0:T(8,128)S(1)} %copy.14), kind=kOutput, calls=%fused_computation.15.clone.1 | convolution fusion | flops 451026944 | bytes 9127937 | tf_op jit(solution)/shard_map/while/body/eval_jaxpr/dot_general | solution.py:22
  214.8 8.9 %fusion.103 = f32[4096,512]{1,0:T(8,128)} fusion(f32[32,4096]{1,0:T(8,128)S(1)} %get-tuple-element.113, f32[49,512]{1,0:T(8,128)S(1)} %copy.14), kind=kOutput, calls=%fused_computation.24.clone.1 | convolution fusion | flops 805306368 | bytes 8978432 | tf_op jit(solution)/shard_map/while/body/eval_jaxpr/dot_general | solution.py:38
  223.8 14.8 %fusion.104 = f32[17,4096]{1,0:T(8,128)S(1)} fusion(f32[4096,512]{1,0:T(8,128)} %fusion.103, f32[512]{0:T(512)S(1)} %multiply_reduce_fusion.4, f32[4096]{0:T(1024)S(1)} %get-tuple-element.112, f32[17,4096]{1,0:T(8,128)S(1)} %get-tuple-element.104, pred[]{:T(512)S(6)} %compare.15, f32[49,512]{1,0:T(8,128)S(1)} %copy.14), kind=kOutput, calls=%fused_computation.15.clone.1 | convolution fusion | flops 451026944 | bytes 9127937 | tf_op jit(solution)/shard_map/while/body/eval_jaxpr/dot_general | solution.py:22
  240.7 8.9 %fusion.103 = f32[4096,512]{1,0:T(8,128)} fusion(f32[32,4096]{1,0:T(8,128)S(1)} %get-tuple-element.113, f32[49,512]{1,0:T(8,128)S(1)} %copy.14), kind=kOutput, calls=%fused_computation.24.clone.1 | convolution fusion | flops 805306368 | bytes 8978432 | tf_op jit(solution)/shard_map/while/body/eval_jaxpr/dot_general | solution.py:38
  249.6 14.8 %fusion.104 = f32[17,4096]{1,0:T(8,128)S(1)} fusion(f32[4096,512]{1,0:T(8,128)} %fusion.103, f32[512]{0:T(512)S(1)} %multiply_reduce_fusion.4, f32[4096]{0:T(1024)S(1)} %get-tuple-element.112, f32[17,4096]{1,0:T(8,128)S(1)} %get-tuple-element.104, pred[]{:T(512)S(6)} %compare.15, f32[49,512]{1,0:T(8,128)S(1)} %copy.14), kind=kOutput, calls=%fused_computation.15.clone.1 | convolution fusion | flops 451026944 | bytes 9127937 | tf_op jit(solution)/shard_map/while/body/eval_jaxpr/dot_general | solution.py:22
  264.6 8.9 %fusion.103 = f32[4096,512]{1,0:T(8,128)} fusion(f32[32,4096]{1,0:T(8,128)S(1)} %get-tuple-element.113, f32[49,512]{1,0:T(8,128)S(1)} %copy.14), kind=kOutput, calls=%fused_computation.24.clone.1 | convolution fusion | flops 805306368 | bytes 8978432 | tf_op jit(solution)/shard_map/while/body/eval_jaxpr/dot_general | solution.py:38
  273.5 14.8 %fusion.104 = f32[17,4096]{1,0:T(8,128)S(1)} fusion(f32[4096,512]{1,0:T(8,128)} %fusion.103, f32[512]{0:T(512)S(1)} %multiply_reduce_fusion.4, f32[4096]{0:T(1024)S(1)} %get-tuple-element.112, f32[17,4096]{1,0:T(8,128)S(1)} %get-tuple-element.104, pred[]{:T(512)S(6)} %compare.15, f32[49,512]{1,0:T(8,128)S(1)} %copy.14), kind=kOutput, calls=%fused_computation.15.clone.1 | convolution fusion | flops 451026944 | bytes 9127937 | tf_op jit(solution)/shard_map/while/body/eval_jaxpr/dot_general | solution.py:22
  290.4 8.9 %fusion.103 = f32[4096,512]{1,0:T(8,128)} fusion(f32[32,4096]{1,0:T(8,128)S(1)} %get-tuple-element.113, f32[49,512]{1,0:T(8,128)S(1)} %copy.14), kind=kOutput, calls=%fused_computation.24.clone.1 | convolution fusion | flops 805306368 | bytes 8978432 | tf_op jit(solution)/shard_map/while/body/eval_jaxpr/dot_general | solution.py:38
  299.3 14.8 %fusion.104 = f32[17,4096]{1,0:T(8,128)S(1)} fusion(f32[4096,512]{1,0:T(8,128)} %fusion.103, f32[512]{0:T(512)S(1)} %multiply_reduce_fusion.4, f32[4096]{0:T(1024)S(1)} %get-tuple-element.112, f32[17,4096]{1,0:T(8,128)S(1)} %get-tuple-element.104, pred[]{:T(512)S(6)} %compare.15, f32[49,512]{1,0:T(8,128)S(1)} %copy.14), kind=kOutput, calls=%fused_computation.15.clone.1 | convolution fusion | flops 451026944 | bytes 9127937 | tf_op jit(solution)/shard_map/while/body/eval_jaxpr/dot_general | solution.py:22
  323.2 14.8 %fusion.104 = f32[17,4096]{1,0:T(8,128)S(1)} fusion(f32[4096,512]{1,0:T(8,128)} %fusion.103, f32[512]{0:T(512)S(1)} %multiply_reduce_fusion.4, f32[4096]{0:T(1024)S(1)} %get-tuple-element.112, f32[17,4096]{1,0:T(8,128)S(1)} %get-tuple-element.104, pred[]{:T(512)S(6)} %compare.15, f32[49,512]{1,0:T(8,128)S(1)} %copy.14), kind=kOutput, calls=%fused_computation.15.clone.1 | convolution fusion | flops 451026944 | bytes 9127937 | tf_op jit(solution)/shard_map/while/body/eval_jaxpr/dot_general | solution.py:22
  348.7 14.8 %fusion.104 = f32[17,4096]{1,0:T(8,128)S(1)} fusion(f32[4096,512]{1,0:T(8,128)} %fusion.103, f32[512]{0:T(512)S(1)} %multiply_reduce_fusion.4, f32[4096]{0:T(1024)S(1)} %get-tuple-element.112, f32[17,4096]{1,0:T(8,128)S(1)} %get-tuple-element.104, pred[]{:T(512)S(6)} %compare.15, f32[49,512]{1,0:T(8,128)S(1)} %copy.14), kind=kOutput, calls=%fused_computation.15.clone.1 | convolution fusion | flops 451026944 | bytes 9127937 | tf_op jit(solution)/shard_map/while/body/eval_jaxpr/dot_general | solution.py:22
  372.6 14.8 %fusion.104 = f32[17,4096]{1,0:T(8,128)S(1)} fusion(f32[4096,512]{1,0:T(8,128)} %fusion.103, f32[512]{0:T(512)S(1)} %multiply_reduce_fusion.4, f32[4096]{0:T(1024)S(1)} %get-tuple-element.112, f32[17,4096]{1,0:T(8,128)S(1)} %get-tuple-element.104, pred[]{:T(512)S(6)} %compare.15, f32[49,512]{1,0:T(8,128)S(1)} %copy.14), kind=kOutput, calls=%fused_computation.15.clone.1 | convolution fusion | flops 451026944 | bytes 9127937 | tf_op jit(solution)/shard_map/while/body/eval_jaxpr/dot_general | solution.py:22
  396.5 14.8 %fusion.104 = f32[17,4096]{1,0:T(8,128)S(1)} fusion(f32[4096,512]{1,0:T(8,128)} %fusion.103, f32[512]{0:T(512)S(1)} %multiply_reduce_fusion.4, f32[4096]{0:T(1024)S(1)} %get-tuple-element.112, f32[17,4096]{1,0:T(8,128)S(1)} %get-tuple-element.104, pred[]{:T(512)S(6)} %compare.15, f32[49,512]{1,0:T(8,128)S(1)} %copy.14), kind=kOutput, calls=%fused_computation.15.clone.1 | convolution fusion | flops 451026944 | bytes 9127937 | tf_op jit(solution)/shard_map/while/body/eval_jaxpr/dot_general | solution.py:22
  418.3 13.0 %fusion.49 = f32[17,4096]{1,0:T(8,128)} fusion(f32[17,4096]{1,0:T(8,128)S(1)} %get-tuple-element.32, f32[4096,512]{1,0:T(8,128)S(1)} %fusion.59, f32[512]{0:T(512)S(1)} %multiply_reduce_fusion.2, f32[4096]{0:T(1024)S(1)} %get-tuple-element.123, f32[49,512]{1,0:T(8,128)S(1)} %get-tuple-element.33), kind=kOutput, calls=%fused_computation.46 | convolution fusion | flops 450957312 | bytes 9127936 | tf_op jit(solution)/shard_map/dot_general | solution.py:22
  432.2 32.4 %reduce-scatter.2.cloned.1.call-done = f32[17,512]{1,0:T(8,128)} async-done(((f32[17,4096]{1,0:T(8,128)}), f32[17,512]{1,0:T(8,128)}) %reduce-scatter.2.cloned.1.call-update) | async-done | bytes 34832 | tf_op jit(solution)/shard_map/reduce_scatter | solution.py:54
  465.6 68.2 %all-reduce = (f32[17,17]{1,0:T(8,128)S(1)}, f32[17,17]{0,1:T(8,128)S(1)}) all-reduce(f32[17,17]{1,0:T(8,128)S(1)} %fusion.77, f32[17,17]{0,1:T(8,128)S(1)} %convolution_bitcast_fusion), channel_id=1, replica_groups=mesh['blk'=16,'narrow'=8] {'blk','narrow'}, use_global_device_ids=true, to_apply=%region_9.10 | all-reduce | flops 578 | bytes 4624 | tf_op jit(solution)/shard_map/psum | solution.py:56
  540.5 64.6 %psum.23 = f32[17,17]{1,0:T(8,128)S(1)} all-reduce(f32[17,17]{1,0:T(8,128)S(1)} %fusion.62), channel_id=1, replica_groups=mesh['blk'=16,'narrow'=8] {'blk','narrow'}, use_global_device_ids=true, to_apply=%region_10.12 | all-reduce | flops 289 | bytes 2312 | tf_op jit(solution)/shard_map/psum | solution.py:62
  (97 shorter events, 75.0 us)
Async XLA Ops:
  7.2 457.4 %reduce-scatter.2.cloned.1.call-start = ((), (), s32[]{:S(2)}) async-start(), calls=%async_computation.1 | async-start | bytes 442368 | tf_op jit(solution)/shard_map/reduce_scatter | solution.py:54
  34.6 31.6 %collective-permute-start = (f32[49,512]{1,0:T(8,128)S(1)}, f32[49,512]{1,0:T(8,128)S(1)}, u32[]{:S(2)}, u32[]{:S(2)}) collective-permute-start(f32[49,512]{1,0:T(8,128)S(1)} %copy.14), channel_id=1, source_target_pairs={{120,0},{0,8},{8,16},{16,24},{24,32},{32,40},{40,48},{48,56},{56,6... | collective-permute-start | bytes 301064 | tf_op jit(solution)/shard_map/while/body/eval_jaxpr/ppermute | solution.py:12
  66.2 23.8 %collective-permute-start = (f32[49,512]{1,0:T(8,128)S(1)}, f32[49,512]{1,0:T(8,128)S(1)}, u32[]{:S(2)}, u32[]{:S(2)}) collective-permute-start(f32[49,512]{1,0:T(8,128)S(1)} %copy.14), channel_id=1, source_target_pairs={{120,0},{0,8},{8,16},{16,24},{24,32},{32,40},{40,48},{48,56},{56,6... | collective-permute-start | bytes 301064 | tf_op jit(solution)/shard_map/while/body/eval_jaxpr/ppermute | solution.py:12
  90.1 25.8 %collective-permute-start = (f32[49,512]{1,0:T(8,128)S(1)}, f32[49,512]{1,0:T(8,128)S(1)}, u32[]{:S(2)}, u32[]{:S(2)}) collective-permute-start(f32[49,512]{1,0:T(8,128)S(1)} %copy.14), channel_id=1, source_target_pairs={{120,0},{0,8},{8,16},{16,24},{24,32},{32,40},{40,48},{48,56},{56,6... | collective-permute-start | bytes 301064 | tf_op jit(solution)/shard_map/while/body/eval_jaxpr/ppermute | solution.py:12
  115.9 23.8 %collective-permute-start = (f32[49,512]{1,0:T(8,128)S(1)}, f32[49,512]{1,0:T(8,128)S(1)}, u32[]{:S(2)}, u32[]{:S(2)}) collective-permute-start(f32[49,512]{1,0:T(8,128)S(1)} %copy.14), channel_id=1, source_target_pairs={{120,0},{0,8},{8,16},{16,24},{24,32},{32,40},{40,48},{48,56},{56,6... | collective-permute-start | bytes 301064 | tf_op jit(solution)/shard_map/while/body/eval_jaxpr/ppermute | solution.py:12
  139.8 25.5 %collective-permute-start = (f32[49,512]{1,0:T(8,128)S(1)}, f32[49,512]{1,0:T(8,128)S(1)}, u32[]{:S(2)}, u32[]{:S(2)}) collective-permute-start(f32[49,512]{1,0:T(8,128)S(1)} %copy.14), channel_id=1, source_target_pairs={{120,0},{0,8},{8,16},{16,24},{24,32},{32,40},{40,48},{48,56},{56,6... | collective-permute-start | bytes 301064 | tf_op jit(solution)/shard_map/while/body/eval_jaxpr/ppermute | solution.py:12
  165.4 23.8 %collective-permute-start = (f32[49,512]{1,0:T(8,128)S(1)}, f32[49,512]{1,0:T(8,128)S(1)}, u32[]{:S(2)}, u32[]{:S(2)}) collective-permute-start(f32[49,512]{1,0:T(8,128)S(1)} %copy.14), channel_id=1, source_target_pairs={{120,0},{0,8},{8,16},{16,24},{24,32},{32,40},{40,48},{48,56},{56,6... | collective-permute-start | bytes 301064 | tf_op jit(solution)/shard_map/while/body/eval_jaxpr/ppermute | solution.py:12
  189.2 25.4 %collective-permute-start = (f32[49,512]{1,0:T(8,128)S(1)}, f32[49,512]{1,0:T(8,128)S(1)}, u32[]{:S(2)}, u32[]{:S(2)}) collective-permute-start(f32[49,512]{1,0:T(8,128)S(1)} %copy.14), channel_id=1, source_target_pairs={{120,0},{0,8},{8,16},{16,24},{24,32},{32,40},{40,48},{48,56},{56,6... | collective-permute-start | bytes 301064 | tf_op jit(solution)/shard_map/while/body/eval_jaxpr/ppermute | solution.py:12
  214.7 23.8 %collective-permute-start = (f32[49,512]{1,0:T(8,128)S(1)}, f32[49,512]{1,0:T(8,128)S(1)}, u32[]{:S(2)}, u32[]{:S(2)}) collective-permute-start(f32[49,512]{1,0:T(8,128)S(1)} %copy.14), channel_id=1, source_target_pairs={{120,0},{0,8},{8,16},{16,24},{24,32},{32,40},{40,48},{48,56},{56,6... | collective-permute-start | bytes 301064 | tf_op jit(solution)/shard_map/while/body/eval_jaxpr/ppermute | solution.py:12
  238.6 25.8 %collective-permute-start = (f32[49,512]{1,0:T(8,128)S(1)}, f32[49,512]{1,0:T(8,128)S(1)}, u32[]{:S(2)}, u32[]{:S(2)}) collective-permute-start(f32[49,512]{1,0:T(8,128)S(1)} %copy.14), channel_id=1, source_target_pairs={{120,0},{0,8},{8,16},{16,24},{24,32},{32,40},{40,48},{48,56},{56,6... | collective-permute-start | bytes 301064 | tf_op jit(solution)/shard_map/while/body/eval_jaxpr/ppermute | solution.py:12
  264.4 23.8 %collective-permute-start = (f32[49,512]{1,0:T(8,128)S(1)}, f32[49,512]{1,0:T(8,128)S(1)}, u32[]{:S(2)}, u32[]{:S(2)}) collective-permute-start(f32[49,512]{1,0:T(8,128)S(1)} %copy.14), channel_id=1, source_target_pairs={{120,0},{0,8},{8,16},{16,24},{24,32},{32,40},{40,48},{48,56},{56,6... | collective-permute-start | bytes 301064 | tf_op jit(solution)/shard_map/while/body/eval_jaxpr/ppermute | solution.py:12
  288.3 25.8 %collective-permute-start = (f32[49,512]{1,0:T(8,128)S(1)}, f32[49,512]{1,0:T(8,128)S(1)}, u32[]{:S(2)}, u32[]{:S(2)}) collective-permute-start(f32[49,512]{1,0:T(8,128)S(1)} %copy.14), channel_id=1, source_target_pairs={{120,0},{0,8},{8,16},{16,24},{24,32},{32,40},{40,48},{48,56},{56,6... | collective-permute-start | bytes 301064 | tf_op jit(solution)/shard_map/while/body/eval_jaxpr/ppermute | solution.py:12
  314.2 23.8 %collective-permute-start = (f32[49,512]{1,0:T(8,128)S(1)}, f32[49,512]{1,0:T(8,128)S(1)}, u32[]{:S(2)}, u32[]{:S(2)}) collective-permute-start(f32[49,512]{1,0:T(8,128)S(1)} %copy.14), channel_id=1, source_target_pairs={{120,0},{0,8},{8,16},{16,24},{24,32},{32,40},{40,48},{48,56},{56,6... | collective-permute-start | bytes 301064 | tf_op jit(solution)/shard_map/while/body/eval_jaxpr/ppermute | solution.py:12
  338.0 25.5 %collective-permute-start = (f32[49,512]{1,0:T(8,128)S(1)}, f32[49,512]{1,0:T(8,128)S(1)}, u32[]{:S(2)}, u32[]{:S(2)}) collective-permute-start(f32[49,512]{1,0:T(8,128)S(1)} %copy.14), channel_id=1, source_target_pairs={{120,0},{0,8},{8,16},{16,24},{24,32},{32,40},{40,48},{48,56},{56,6... | collective-permute-start | bytes 301064 | tf_op jit(solution)/shard_map/while/body/eval_jaxpr/ppermute | solution.py:12
  363.6 23.8 %collective-permute-start = (f32[49,512]{1,0:T(8,128)S(1)}, f32[49,512]{1,0:T(8,128)S(1)}, u32[]{:S(2)}, u32[]{:S(2)}) collective-permute-start(f32[49,512]{1,0:T(8,128)S(1)} %copy.14), channel_id=1, source_target_pairs={{120,0},{0,8},{8,16},{16,24},{24,32},{32,40},{40,48},{48,56},{56,6... | collective-permute-start | bytes 301064 | tf_op jit(solution)/shard_map/while/body/eval_jaxpr/ppermute | solution.py:12
  387.4 23.8 %collective-permute-start = (f32[49,512]{1,0:T(8,128)S(1)}, f32[49,512]{1,0:T(8,128)S(1)}, u32[]{:S(2)}, u32[]{:S(2)}) collective-permute-start(f32[49,512]{1,0:T(8,128)S(1)} %copy.14), channel_id=1, source_target_pairs={{120,0},{0,8},{8,16},{16,24},{24,32},{32,40},{40,48},{48,56},{56,6... | collective-permute-start | bytes 301064 | tf_op jit(solution)/shard_map/while/body/eval_jaxpr/ppermute | solution.py:12
  418.2 13.7 %copy-start = (f32[17,512]{1,0:T(8,128)S(1)}, f32[17,512]{1,0:T(8,128)}, u32[]{:S(2)}) copy-start(f32[17,512]{1,0:T(8,128)} %param.15) | copy-start | bytes 104452
  418.3 13.7 %copy-start.2 = (f32[17,512]{1,0:T(8,128)S(1)}, f32[17,512]{1,0:T(8,128)}, u32[]{:S(2)}) copy-start(f32[17,512]{1,0:T(8,128)} %param.14) | copy-start | bytes 104452
  418.3 188.0 %copy-start.3 = (f32[17,512]{1,0:T(8,128)S(1)}, f32[17,512]{1,0:T(8,128)}, u32[]{:S(2)}) copy-start(f32[17,512]{1,0:T(8,128)} %param.13) | copy-start | bytes 104452
  539.5 67.7 %copy-start.1 = (f32[17,512]{1,0:T(8,128)}, f32[17,512]{1,0:T(8,128)S(1)}, u32[]{:S(2)}) copy-start(f32[17,512]{1,0:T(8,128)S(1)} %convolution_subtract_fusion) | copy-start | bytes 104452
Sparse Core Ops, SparseCore 0:
  431.4 33.1 reduce-scatter.1
where the time goes:
time: 615 us; the launch traced here: 614 us
  matrix products  381 us (62%)
  blocking collectives  158 us (26%)
  waiting for transfers between devices  32.5 us (5%)
  starting transfers between devices  20.2 us (3%)
  between operations  14.8 us (2%)
  other arithmetic  6.35 us (1%)
    dot_general x19, matrix products, gram(): lax.dot_general(left, right, (((1,), (1,)), ((), ())), precision=lax.Prec...  236 us
    dot_general x16, matrix products, visit(): lax.dot_general(block_pts, cols_pts, (((0,), (0,)), ((), ())), precision=hi)  141 us
    psum x1, blocking collectives, on_device(): lax.psum((gram(direction, image), gram(direction, residual)), ('blk', 'na...  68.2 us
    psum x1, blocking collectives, on_device(): update = lax.psum(gram(image, new_residual), ('blk', 'narrow'))  64.6 us
    reduce_scatter x1, waiting for transfers between devices, on_device(): summed = lax.psum_scatter(acc, 'narrow', scatter_dimension=1, tiled=True)  32.4 us
    all_gather x1, blocking collectives, on_device(): block_pts = lax.all_gather(scaled, 'narrow', axis=1, tiled=True)  25.5 us
    ppermute x15, starting transfers between devices, from_behind(): return lax.ppermute(block, axis, route)  20.2 us
  transfers between devices with their start and end apart: 16, of which 1 were waited for; matrix products, arithmetic and copies ran while one was open for 58% of the time, Pallas kernels for 0%

commit v1 on v0

v1 whole, which is shorter than its diff:
```python
import functools
import math

import jax
import jax.numpy as jnp
from jax import lax
from jax.experimental import pallas as pl
from jax.experimental.pallas import tpu as pltpu
from jax.sharding import PartitionSpec as P

BF16 = jnp.bfloat16
F32 = jnp.float32
LN2 = math.log(2.0)
MESH = pl.DeviceIdType.MESH
FEATS = 32
SIDES = 17
SIDES_PAD = 24
PTS = 512
BLK = 16
NARROW = 8
HALF = BLK // 2
PACKET = 56
DEPTH = 256
CHUNK = 2048


def dot(left, right, dims=((1,), (0,))):
    return lax.dot_general(left, right, (dims, ((), ())), preferred_element_type=F32)


def exact_dot(left, right, dims=((1,), (0,))):
    return lax.dot_general(
        left, right, (dims, ((), ())), precision=lax.Precision.HIGHEST, preferred_element_type=F32
    )


def split3(x):
    first = x.astype(BF16).astype(F32)
    second = (x - first).astype(BF16).astype(F32)
    third = (x - first - second).astype(BF16).astype(F32)
    return first, second, third


def norm_rows(squares, norms_first):
    s1, s2, s3 = split3(squares)
    row = lax.broadcasted_iota(jnp.int32, (16, PTS), 0)
    zero = jnp.zeros((16, PTS), F32)
    base = 0 if norms_first else 3
    ones = 3 if norms_first else 0
    out = jnp.where((row >= ones) & (row < ones + 3), 1.0, zero)
    for place, part in enumerate((s1, s2, s3)):
        out = jnp.where(row == base + place, jnp.broadcast_to(part, (16, PTS)), out)
    return out


def expand(pts, left):
    p1, p2, p3 = split3(pts)
    squares = jnp.sum(pts * pts, 0, keepdims=True)
    order = (p1, p1, p2, p2, p1, p3) if left else (p1, p2, p1, p2, p3, p1)
    scale = -2.0 if left else 1.0
    rows = [part * scale for part in order]
    rows.append(norm_rows(squares, left))
    rows.append(jnp.zeros((DEPTH - 6 * FEATS - 16, PTS), F32))
    return jnp.concatenate(rows, 0)


def split_dir(rows):
    hi = rows.astype(BF16).astype(F32)
    return jnp.concatenate([hi, rows - hi], 0).astype(BF16)


def matern(q):
    q = jnp.maximum(q, 1e-30)
    t = q * lax.rsqrt(q)
    s = t + 1.5 / LN2
    return (s * s + 0.75 / LN2**2) * jnp.exp2(-t)


def kernel(points, scale, noise, solution, residual, direction, new_solution, new_residual, new_direction,
           pkt, gat, cols, left, ldir, right, rdir, fwd, back, rsend, rrecv, bsend, brecv, dir24, res24, img24,
           gram, ar1, ar2, own,
           gat_send, gat_recv, col_send, col_recv, r_send, r_recv, b_send, b_recv,
           ar1_send, ar1_recv, ar2_send, ar2_recv):
    b = lax.axis_index("blk")
    n = lax.axis_index("narrow")

    def narrow_peer(offset):
        return (b, lax.rem(n + offset, NARROW))

    def blk_peer(offset):
        return (lax.rem(b + offset, BLK), n)

    barrier = pltpu.get_barrier_semaphore()
    for j in range(1, NARROW):
        pl.semaphore_signal(barrier, inc=1, device_id=narrow_peer(j), device_id_type=MESH)
    for k in range(1, BLK):
        pl.semaphore_signal(barrier, inc=1, device_id=blk_peer(k), device_id_type=MESH)

    dir24[...] = jnp.zeros_like(dir24)
    dir24[0:SIDES, :] = direction[...]
    res24[...] = jnp.zeros_like(res24)
    res24[0:SIDES, :] = residual[...]
    pkt[0:FEATS, :] = points[...] * scale[...]
    pkt[FEATS:PACKET, :] = dir24[...]
    pl.semaphore_wait(barrier, NARROW + BLK - 2)

    def gather_copy(j):
        return pltpu.make_async_remote_copy(
            src_ref=pkt, dst_ref=gat.at[j], send_sem=gat_send.at[j], recv_sem=gat_recv.at[j],
            device_id=narrow_peer(NARROW - j), device_id_type=MESH)

    def column_copy(k):
        return pltpu.make_async_remote_copy(
            src_ref=pkt, dst_ref=cols.at[k], send_sem=col_send.at[k], recv_sem=col_recv.at[k],
            device_id=blk_peer(BLK - k), device_id_type=MESH)

    def forward_copy(k):
        return pltpu.make_async_remote_copy(
            src_ref=rsend.at[k], dst_ref=rrecv.at[k], send_sem=r_send.at[k], recv_sem=r_recv.at[k],
            device_id=blk_peer(k), device_id_type=MESH)

    def back_copy(j):
        return pltpu.make_async_remote_copy(
            src_ref=bsend.at[j], dst_ref=brecv.at[j], send_sem=b_send.at[j], recv_sem=b_recv.at[j],
            device_id=narrow_peer(j), device_id_type=MESH)

    for j in range(1, NARROW):
        gather_copy(j).start()
    for k in range(1, HALF + 1):
        column_copy(k).start()

    def load_right(packet):
        right[...] = expand(packet[0:FEATS, :], False).astype(BF16)
        rdir[...] = split_dir(packet[FEATS:PACKET, :])

    def load_left(j, packet):
        at = pl.ds(pl.multiple_of(j * PTS, PTS), PTS)
        left[at, :] = expand(packet[0:FEATS, :], True).T.astype(BF16)
        ldir[:, at] = split_dir(packet[FEATS:PACKET, :])

    def tile(start, size):
        at = pl.ds(pl.multiple_of(start, PTS), size)
        kern = matern(dot(left[at, :], right[...]))
        hi = kern.astype(BF16)
        lo = (kern - hi.astype(F32)).astype(BF16)
        sides = ldir[:, at]
        fwd[...] += dot(sides, hi) + dot(sides, lo)
        back[at, :] += dot(hi, rdir[...], ((1,), (1,))) + dot(lo, rdir[...], ((1,), (1,)))

    back[...] = jnp.zeros_like(back)
    fwd[...] = jnp.zeros_like(fwd)
    load_right(pkt)
    load_left(0, pkt)
    tile(0, PTS)

    @pl.loop(1, NARROW)
    def _(j):
        gather_copy(j).wait_recv()
        load_left(j, gat.at[j])

        @pl.when(j <= NARROW // 2)
        def _():
            tile(j * PTS, PTS)

    own[...] = fwd[0:SIDES_PAD, :] + fwd[SIDES_PAD:, :]
    back[0:PTS, :] = jnp.zeros((PTS, 2 * SIDES_PAD), F32)
    back[NARROW // 2 * PTS:(NARROW // 2 + 1) * PTS, :] = jnp.zeros((PTS, 2 * SIDES_PAD), F32)

    upper = jnp.where(b >= HALF, PTS, 0)

    @pl.loop(1, HALF + 1)
    def _(k):
        column_copy(k).wait_recv()
        load_right(cols.at[k])
        fwd[...] = jnp.zeros_like(fwd)
        tile(jnp.where(k == HALF, upper, 0), CHUNK)

        @pl.when(k < HALF)
        def _():
            tile(CHUNK, CHUNK)

        rsend[k] = fwd[0:SIDES_PAD, :] + fwd[SIDES_PAD:, :]
        forward_copy(k).start()

    def back_slice(j):
        part = back[pl.ds(pl.multiple_of(j * PTS, PTS), PTS), :].T
        return part[0:SIDES_PAD, :] + part[SIDES_PAD:, :]

    @pl.loop(1, NARROW)
    def _(j):
        bsend[j] = back_slice(j)
        back_copy(j).start()

    own[...] += back_slice(0)
    for k in range(1, HALF + 1):
        forward_copy(k).wait_recv()
        own[...] += rrecv[k]
    for j in range(1, NARROW):
        back_copy(j).wait_recv()
        own[...] += brecv[j]
    img24[...] = own[...] * (LN2 * LN2 / 3.0) + noise[...] * dir24[...]

    zeros8 = jnp.zeros((8, PTS), F32)
    zeros64 = jnp.zeros((64, PTS), F32)
    img, dirs, res = img24[...], dir24[...], res24[...]
    table = jnp.concatenate([dirs, zeros8, img, zeros8, zeros64], 0)
    other = jnp.concatenate([zeros64, img, zeros8, dirs, zeros8], 0)
    gram[...] = exact_dot(img, table, ((1,), (1,))) + exact_dot(res, other, ((1,), (1,)))

    def ar1_copy(j):
        return pltpu.make_async_remote_copy(
            src_ref=gram, dst_ref=ar1.at[n], send_sem=ar1_send.at[j], recv_sem=ar1_recv.at[j],
            device_id=narrow_peer(j), device_id_type=MESH)

    for j in range(1, NARROW):
        ar1_copy(j).start()
    ar1[n] = gram[...]
    for j in range(1, NARROW):
        ar1_copy(j).wait()
    total = ar1[0]
    for j in range(1, NARROW):
        total = total + ar1[j]
    gram[...] = total

    def ar2_copy(k):
        return pltpu.make_async_remote_copy(
            src_ref=gram, dst_ref=ar2.at[b], send_sem=ar2_send.at[k], recv_sem=ar2_recv.at[k],
            device_id=blk_peer(k), device_id_type=MESH)

    for k in range(1, BLK):
        ar2_copy(k).start()
    ar2[b] = gram[...]
    for k in range(1, BLK):
        ar2_copy(k).wait()
    total = ar2[0]
    for k in range(1, BLK):
        total = total + ar2[k]

    curv = total[:, 0:SIDES_PAD]
    curv = 0.5 * (curv + curv.T)
    outer = pltpu.roll(total, 96, 1)[:, 0:SIDES_PAD]
    img_res = pltpu.roll(total, 64, 1)[:, 0:SIDES_PAD]
    dir_res = pltpu.roll(total, 32, 1)[:, 0:SIDES_PAD]
    row = lax.broadcasted_iota(jnp.int32, (SIDES_PAD, SIDES_PAD), 0)
    col = lax.broadcasted_iota(jnp.int32, (SIDES_PAD, SIDES_PAD), 1)
    inverse = (row == col).astype(F32)
    for i in range(SIDES):
        pivot = 1.0 / curv[i:i + 1, i:i + 1]
        head = curv[i:i + 1, :] * pivot
        tail = inverse[i:i + 1, :] * pivot
        factor = jnp.where(row[:, 0:1] == i, 0.0, curv[:, i:i + 1])
        curv = jnp.where(row == i, head, curv - factor * head)
        inverse = jnp.where(row == i, tail, inverse - factor * tail)

    step_t = exact_dot(dir_res, inverse)
    conj_t = exact_dot(exact_dot(step_t, outer) - img_res, inverse)
    res_new = res - exact_dot(step_t, img)
    new_solution[...] = solution[...] + exact_dot(step_t, dirs)[0:SIDES, :]
    new_residual[...] = res_new[0:SIDES, :]
    new_direction[...] = (res_new + exact_dot(conj_t, dirs))[0:SIDES, :]

    for j in range(1, NARROW):
        gather_copy(j).wait_send()
        back_copy(j).wait_send()
    for k in range(1, HALF + 1):
        column_copy(k).wait_send()
        forward_copy(k).wait_send()


def on_device(points, lengthscale, noise, solution, residual, direction):
    scale = (math.sqrt(5.0) / LN2 / lengthscale)[:, None]
    vmem = pl.BlockSpec(memory_space=pltpu.VMEM)
    sem = pltpu.SemaphoreType.DMA
    rows = NARROW * PTS
    return pl.pallas_call(
        kernel,
        out_shape=[jax.ShapeDtypeStruct((SIDES, PTS), F32)] * 3,
        in_specs=[vmem] * 6,
        out_specs=[vmem] * 3,
        scratch_shapes=[
            pltpu.VMEM((PACKET, PTS), F32),
            pltpu.VMEM((NARROW, PACKET, PTS), F32),
            pltpu.VMEM((HALF + 1, PACKET, PTS), F32),
            pltpu.VMEM((rows, DEPTH), BF16),
            pltpu.VMEM((2 * SIDES_PAD, rows), BF16),
            pltpu.VMEM((DEPTH, PTS), BF16),
            pltpu.VMEM((2 * SIDES_PAD, PTS), BF16),
            pltpu.VMEM((2 * SIDES_PAD, PTS), F32),
            pltpu.VMEM((rows, 2 * SIDES_PAD), F32),
            pltpu.VMEM((HALF + 1, SIDES_PAD, PTS), F32),
            pltpu.VMEM((HALF + 1, SIDES_PAD, PTS), F32),
            pltpu.VMEM((NARROW, SIDES_PAD, PTS), F32),
            pltpu.VMEM((NARROW, SIDES_PAD, PTS), F32),
            pltpu.VMEM((SIDES_PAD, PTS), F32),
            pltpu.VMEM((SIDES_PAD, PTS), F32),
            pltpu.VMEM((SIDES_PAD, PTS), F32),
            pltpu.VMEM((SIDES_PAD, 128), F32),
            pltpu.VMEM((NARROW, SIDES_PAD, 128), F32),
            pltpu.VMEM((BLK, SIDES_PAD, 128), F32),
            pltpu.VMEM((SIDES_PAD, PTS), F32),
            sem((NARROW,)), sem((NARROW,)), sem((HALF + 1,)), sem((HALF + 1,)),
            sem((HALF + 1,)), sem((HALF + 1,)), sem((NARROW,)), sem((NARROW,)),
            sem((NARROW,)), sem((NARROW,)), sem((BLK,)), sem((BLK,)),
        ],
        compiler_params=pltpu.CompilerParams(
            collective_id=0, has_side_effects=True, vmem_limit_bytes=56 * 2**20
        ),
        cost_estimate=pl.CostEstimate(flops=30_000_000_000, bytes_accessed=1_000_000, transcendentals=34_000_000),
        name="block_cg",
    )(points, scale, noise.reshape(1, 1), solution, residual, direction)


def solution(mesh):
    placed = P(None, ("blk", "narrow"))
    return jax.shard_map(
        on_device,
        mesh=mesh,
        in_specs=(placed, P(), P(), placed, placed, placed),
        out_specs=(placed, placed, placed),
        check_vma=False,
    )
```

time: 615 us -> 107 us (0.17)
  matrix products: 381 us -> 0 us
  blocking collectives: 158 us -> 0 us
  Pallas kernels: 0 us -> 101 us
  waiting for transfers between devices: 32.5 us -> 0 us
  starting transfers between devices: 20.2 us -> 0 us
  between operations: 14.8 us -> 1.31 us
  other arithmetic: 6.35 us -> 0.01 us
    dot_general x38 -> x0, matrix products: 380 us -> none  [the longest x19 236 us: gram(): lax.dot_general(left, right, (((1,), (1,)), ((), ())), precision=lax.Prec...]
    psum x2 -> x0, blocking collectives: 133 us -> none  [the longest x1 68.2 us: on_device(): lax.psum((gram(direction, image), gram(direction, residual)), ('blk', 'na...]
    pallas_call x0 -> x1, Pallas kernels: none -> 101 us  [on_device(): pl.pallas_call(kernel, out_shape=[jax.ShapeDtypeStruct((SIDES, PTS), F32)...]
    reduce_scatter x1 -> x0, waiting for transfers between devices: 32.4 us -> none  [on_device(): summed = lax.psum_scatter(acc, 'narrow', scatter_dimension=1, tiled=True)]
    all_gather x1 -> x0, blocking collectives: 25.5 us -> none  [on_device(): block_pts = lax.all_gather(scaled, 'narrow', axis=1, tiled=True)]
    ppermute x15 -> x0, starting transfers between devices: 20.2 us -> none  [from_behind(): return lax.ppermute(block, axis, route)]
  transfers between devices with their start and end apart: 16 -> 0, of which waited for: 1 -> 0; matrix products, arithmetic and copies ran while one was open for 58% -> 0% of each run, Pallas kernels for 0% -> 0%
where the time goes in v1:
time: 107 us
  Pallas kernels  101 us (94%)
  local copies, waits for them, and re-layouts  4.22 us (4%)
  between operations  1.31 us (1%)
    pallas_call x1, Pallas kernels, on_device(): pl.pallas_call(kernel, out_shape=[jax.ShapeDtypeStruct((SIDES, PTS), F32)...  101 us
    unnamed x9, local copies, waits for them, and re-layouts  3.52 us

profile of v1, /device:TPU:1, one launch (start us, length us, event | category | flops | bytes accessed | tf_op | source)
XLA Modules:
  0.0 106.7 jit_solution(4793870014856416110)
XLA Ops:
  1.3 0.0 copy-start.2
  1.3 0.6 copy-done.2
  1.9 0.7 copy.9.scale
  2.6 101.1 %block_cg.1 = (f32[17,512]{1,0:T(8,128)}, f32[17,512]{1,0:T(8,128)}, f32[17,512]{1,0:T(8,128)}) custom-call(f32[32,512]{1,0:T(8,128)} %points.1, f32[32,1]{1,0:T(8,128)} %copy.9.scale, f32[1,1]{1,0:T(1,128)} %bitcast.3.noise, f32[17,512]{1,0:T(8,128)} %solution.1, f32[17,512]{1,0:T(8,128)} %residual.1, f32[17,512]{1,0:T(8,128)} %direction.1), custom_call_target="tpu_custom_call" | custom-call | flops 30000001024 | bytes 1000000 | tf_op jit(solution)/shard_map/block_cg/pallas_call | solution.py:275
  103.8 0.0 copy-start.1
  103.8 1.4 %copy.14 = f32[17,512]{1,0:T(8,128)} copy(f32[17,512]{1,0:T(8,128)} %get-tuple-element.6) | data formatting | bytes 69632
  105.2 0.0 copy-done.1
  105.2 0.0 copy-start
  105.2 0.6 copy.15
  105.9 0.2 copy-done
  106.1 0.6 copy.16
  (1 shorter events, 0.0 us)
Async XLA Ops:
  1.3 0.7 copy-start.2
  103.8 1.4 %copy-start.1 = (f32[17,512]{1,0:T(8,128)S(1)}, f32[17,512]{1,0:T(8,128)}, u32[]{:S(2)}) copy-start(f32[17,512]{1,0:T(8,128)} %get-tuple-element.7) | copy-start | bytes 104452
  105.2 0.8 copy-start

commit v2 on v1

v2 whole, which is shorter than its diff:
```python
import functools
import math

import jax
import jax.numpy as jnp
from jax import lax
from jax.experimental import pallas as pl
from jax.experimental.pallas import tpu as pltpu
from jax.sharding import PartitionSpec as P

BF16 = jnp.bfloat16
F32 = jnp.float32
LN2 = math.log(2.0)
MESH = pl.DeviceIdType.MESH
FEATS = 32
SIDES = 17
SIDES_PAD = 24
PTS = 512
ROWS = 8
PLANE = 16
SIDE = 4
FULL = 6
OFFSETS = ((1, 0), (0, 3), (1, 1), (3, 1), (2, 3), (3, 2), (2, 0), (0, 2), (2, 2))
COLS = len(OFFSETS)
STEP_X = tuple(dx for dx, _ in OFFSETS)
STEP_Z = tuple(dz for _, dz in OFFSETS)
PACKET = 56
DEPTH = 256
CHUNK = 2048
LANES = 128
LOW = 32
BOOST = 14
F8 = jnp.float8_e4m3fn
F8_TOP = 256.0


def dot(left, right, dims=((1,), (0,))):
    return lax.dot_general(left, right, (dims, ((), ())), preferred_element_type=F32)


def exact_dot(left, right, dims=((1,), (0,))):
    return lax.dot_general(
        left, right, (dims, ((), ())), precision=lax.Precision.HIGHEST, preferred_element_type=F32
    )


def split3(x):
    first = x.astype(BF16).astype(F32)
    second = (x - first).astype(BF16).astype(F32)
    third = (x - first - second).astype(BF16).astype(F32)
    return first, second, third


def norm_rows(squares, norms_first):
    s1, s2, s3 = split3(squares)
    row = lax.broadcasted_iota(jnp.int32, (16, PTS), 0)
    zero = jnp.zeros((16, PTS), F32)
    base = 0 if norms_first else 3
    ones = 3 if norms_first else 0
    out = jnp.where((row >= ones) & (row < ones + 3), 1.0, zero)
    for place, part in enumerate((s1, s2, s3)):
        out = jnp.where(row == base + place, jnp.broadcast_to(part, (16, PTS)), out)
    return out


def expand(pts, left):
    p1, p2, p3 = split3(pts)
    squares = jnp.sum(pts * pts, 0, keepdims=True)
    order = (p1, p1, p2, p2, p1, p3) if left else (p1, p2, p1, p2, p3, p1)
    scale = -2.0 if left else 1.0
    rows = [part * scale for part in order]
    rows.append(norm_rows(squares, left))
    rows.append(jnp.zeros((DEPTH - 6 * FEATS - 16, PTS), F32))
    return jnp.concatenate(rows, 0)


def split_dir(rows):
    hi = rows.astype(BF16).astype(F32)
    return jnp.concatenate([hi, rows - hi], 0).astype(BF16)


def matern(q):
    q = jnp.maximum(q, 1e-30)
    t = q * lax.rsqrt(q)
    return ((q + 3.0 / LN2**2) + t * (3.0 / LN2)) * jnp.exp2(BOOST - t)


def pick(k, values):
    if isinstance(k, int):
        return values[k - 1]
    out = values[0]
    for place, value in enumerate(values[1:], 2):
        out = jnp.where(k == place, value, out)
    return out


def kernel(points, scale, noise, solution, residual, direction, new_solution, new_residual, new_direction,
           pkt, gat, cols, left, ldir, ldirf, ldir8, lscale, right, rdir, rdir8, rscale, fwds, back, rsend, rrecv, bsend, brecv, dir24, res24, img24,
           gram, ar1, ar2, own,
           gat_send, gat_recv, col_send, col_recv, r_send, r_recv, b_send, b_recv,
           ar1_send, ar1_recv, ar2_send, ar2_recv):
    b = lax.axis_index("blk")
    n = lax.axis_index("narrow")

    x = b // 8 * 2 + n % 2
    z = b // 2 % SIDE
    m = n // 2 * 2 + b % 2

    def device(x, z, m):
        return (x // 2 * 8 + z * 2 + m % 2, m // 2 * 2 + x % 2)

    def row_peer(j):
        return device(x, z, lax.rem(m + j, ROWS))

    def plane_peer(dx, dz):
        return device(lax.rem(x + dx, SIDE), lax.rem(z + dz, SIDE), m)

    others = [(dx, dz) for dx in range(SIDE) for dz in range(SIDE) if dx or dz]

    barrier = pltpu.get_barrier_semaphore()
    for j in range(1, ROWS):
        pl.semaphore_signal(barrier, inc=1, device_id=row_peer(j), device_id_type=MESH)
    for dx, dz in others:
        pl.semaphore_signal(barrier, inc=1, device_id=plane_peer(dx, dz), device_id_type=MESH)

    dir24[...] = jnp.zeros_like(dir24)
    dir24[0:SIDES, :] = direction[...]
    res24[...] = jnp.zeros_like(res24)
    res24[0:SIDES, :] = residual[...]
    pkt[0:FEATS, :] = points[...] * scale[...]
    pkt[FEATS:PACKET, :] = dir24[...]
    pl.semaphore_wait(barrier, ROWS + PLANE - 2)

    def gather_copy(j):
        return pltpu.make_async_remote_copy(
            src_ref=pkt, dst_ref=gat.at[j], send_sem=gat_send.at[j], recv_sem=gat_recv.at[j],
            device_id=row_peer(ROWS - j), device_id_type=MESH)

    def column_copy(k):
        return pltpu.make_async_remote_copy(
            src_ref=pkt, dst_ref=cols.at[k], send_sem=col_send.at[k], recv_sem=col_recv.at[k],
            device_id=plane_peer(SIDE - pick(k, STEP_X), SIDE - pick(k, STEP_Z)), device_id_type=MESH)

    def forward_copy(k):
        return pltpu.make_async_remote_copy(
            src_ref=rsend.at[k], dst_ref=rrecv.at[k], send_sem=r_send.at[k], recv_sem=r_recv.at[k],
            device_id=plane_peer(pick(k, STEP_X), pick(k, STEP_Z)), device_id_type=MESH)

    def back_copy(j):
        return pltpu.make_async_remote_copy(
            src_ref=bsend.at[j], dst_ref=brecv.at[j], send_sem=b_send.at[j], recv_sem=b_recv.at[j],
            device_id=row_peer(j), device_id_type=MESH)

    middle = ROWS // 2
    for j in range(1, middle + 1):
        gather_copy(j).start()
    for k in range(1, COLS + 1):
        column_copy(k).start()

    def load_right(packet):
        right[...] = expand(packet[0:FEATS, :], False).astype(BF16)
        rows = packet[FEATS:PACKET, :]
        hi = rows.astype(BF16).astype(F32)
        spare = jnp.zeros((LANES - 2 * SIDES_PAD, PTS), F32)
        rdir[...] = jnp.concatenate([hi, rows - hi, spare], 0).T.astype(BF16)
        plain = jnp.concatenate([rows, jnp.zeros((LANES - SIDES_PAD, PTS), F32)], 0).T
        top = jnp.maximum(jnp.max(jnp.abs(plain), 0, keepdims=True), 1e-30)
        rdir8[...] = (plain * (F8_TOP / top)).astype(F8)
        rscale[...] = jnp.broadcast_to(top * (1.0 / F8_TOP), (8, LANES))

    def scale_left(at):
        rows = ldirf[:, at]
        top = jnp.maximum(jnp.max(jnp.abs(rows), 1, keepdims=True), 1e-30)
        ldir8[:, at] = (rows * (F8_TOP / top)).astype(F8)
        lscale[...] = jnp.broadcast_to(top * (1.0 / F8_TOP), (LOW, LANES))

    def load_left(j, packet):
        at = pl.ds(pl.multiple_of(j * PTS, PTS), PTS)
        left[at, :] = expand(packet[0:FEATS, :], True).T.astype(BF16)
        rows = packet[FEATS:PACKET, :]
        ldir[:, at] = split_dir(rows)
        ldirf[:, at] = jnp.concatenate([rows, jnp.zeros((LOW - SIDES_PAD, PTS), F32)], 0)
        return at

    def tile(k, start, size):
        at = pl.ds(pl.multiple_of(start, PTS), size)
        kern = matern(dot(left[at, :], right[...]))
        hi = kern.astype(BF16)
        lo = (kern - hi.astype(F32)).astype(F8)
        back[at, :] += dot(hi, rdir[...])
        back[at, :] += dot(lo, rdir8[...]) * rscale[0:1, :]
        fwds[k] += dot(ldir[:, at], hi)
        fwds[k, 0:LOW] += dot(ldir8[:, at], lo) * lscale[:, 0:1]

    back[...] = jnp.zeros_like(back)
    fwds[...] = jnp.zeros_like(fwds)
    load_right(pkt)

    @pl.loop(0, middle + 1)
    def _(j):
        @pl.when(j > 0)
        def _():
            gather_copy(j).wait_recv()

        @pl.when(j == 0)
        def _():
            gat[0] = pkt[...]

        scale_left(load_left(j, gat.at[j]))
        tile(0, j * PTS, PTS)

    own[...] = fwds[0, 0:SIDES_PAD] + fwds[0, SIDES_PAD:]
    back[0:PTS, :] = jnp.zeros((PTS, LANES), F32)
    back[middle * PTS:(middle + 1) * PTS, :] = jnp.zeros((PTS, LANES), F32)
    scale_left(pl.ds(0, (middle + 1) * PTS))
    upper_x = jnp.where(x >= SIDE // 2, PTS, 0)
    upper_z = jnp.where(z >= SIDE // 2, PTS, 0)

    def back_slice(j):
        part = back[pl.ds(pl.multiple_of(j * PTS, PTS), PTS), :].T
        return part[0:SIDES_PAD, :] + part[SIDES_PAD:2 * SIDES_PAD, :]

    def send_back(first, last):
        @pl.loop(first, last)
        def _(j):
            bsend[j] = back_slice(j)
            back_copy(j).start()

    @pl.loop(0, COLS + FULL)
    def _(s):
        first = s < COLS
        k = jnp.where(first, s + 1, COLS + FULL - s)

        @pl.when(first)
        def _():
            column_copy(k).wait_recv()

        @pl.when((s >= 1) & (s < ROWS - middle))
        def _():
            gather_copy(s + middle).start()

        @pl.when(s == COLS)
        def _():
            @pl.loop(middle + 1, ROWS)
            def _(j):
                gather_copy(j).wait_recv()
                load_left(j, gat.at[j])

            scale_left(pl.ds(middle * PTS, (ROWS - middle) * PTS))
            send_back(1, middle)

        load_right(cols.at[k])
        upper = jnp.where(k == FULL + 2, upper_z, upper_x)
        tile(k, jnp.where(first, jnp.where(k > FULL, upper, 0), CHUNK), CHUNK)

        @pl.when(s >= FULL)
        def _():
            rsend[k] = fwds[k, 0:SIDES_PAD] + fwds[k, SIDES_PAD:]
            forward_copy(k).start()

    send_back(middle, ROWS)

    own[...] += back_slice(0)
    for k in range(1, COLS + 1):
        forward_copy(k).wait_recv()
        own[...] += rrecv[k]
    for j in range(1, ROWS):
        back_copy(j).wait_recv()
        own[...] += brecv[j]
    img24[...] = own[...] * (LN2 * LN2 / 3.0 / 2.0**BOOST) + noise[...] * dir24[...]

    zeros8 = jnp.zeros((8, PTS), F32)
    zeros64 = jnp.zeros((64, PTS), F32)
    img, dirs, res = img24[...], dir24[...], res24[...]
    table = jnp.concatenate([dirs, zeros8, img, zeros8, zeros64], 0)
    other = jnp.concatenate([zeros64, img, zeros8, dirs, zeros8], 0)
    gram[...] = exact_dot(img, table, ((1,), (1,))) + exact_dot(res, other, ((1,), (1,)))

    def ar1_copy(j):
        return pltpu.make_async_remote_copy(
            src_ref=gram, dst_ref=ar1.at[m], send_sem=ar1_send.at[j], recv_sem=ar1_recv.at[j],
            device_id=row_peer(j), device_id_type=MESH)

    for j in range(1, ROWS):
        ar1_copy(j).start()
    ar1[m] = gram[...]
    for j in range(1, ROWS):
        ar1_copy(j).wait()
    total = ar1[0]
    for j in range(1, ROWS):
        total = total + ar1[j]
    gram[...] = total

    place = x * SIDE + z

    def ar2_copy(k):
        dx, dz = others[k]
        return pltpu.make_async_remote_copy(
            src_ref=gram, dst_ref=ar2.at[place], send_sem=ar2_send.at[k], recv_sem=ar2_recv.at[k],
            device_id=plane_peer(dx, dz), device_id_type=MESH)

    for k in range(PLANE - 1):
        ar2_copy(k).start()
    ar2[place] = gram[...]
    for k in range(PLANE - 1):
        ar2_copy(k).wait()
    total = ar2[0]
    for k in range(1, PLANE):
        total = total + ar2[k]

    curv = total[:, 0:SIDES_PAD]
    curv = 0.5 * (curv + curv.T)
    outer = pltpu.roll(total, 96, 1)[:, 0:SIDES_PAD]
    img_res = pltpu.roll(total, 64, 1)[:, 0:SIDES_PAD]
    dir_res = pltpu.roll(total, 32, 1)[:, 0:SIDES_PAD]
    row = lax.broadcasted_iota(jnp.int32, (SIDES_PAD, SIDES_PAD), 0)
    col = lax.broadcasted_iota(jnp.int32, (SIDES_PAD, SIDES_PAD), 1)
    inverse = (row == col).astype(F32)
    for i in range(SIDES):
        pivot = 1.0 / curv[i:i + 1, i:i + 1]
        head = curv[i:i + 1, :] * pivot
        tail = inverse[i:i + 1, :] * pivot
        factor = jnp.where(row[:, 0:1] == i, 0.0, curv[:, i:i + 1])
        curv = jnp.where(row == i, head, curv - factor * head)
        inverse = jnp.where(row == i, tail, inverse - factor * tail)

    step_t = exact_dot(dir_res, inverse)
    conj_t = exact_dot(exact_dot(step_t, outer) - img_res, inverse)
    res_new = res - exact_dot(step_t, img)
    new_solution[...] = solution[...] + exact_dot(step_t, dirs)[0:SIDES, :]
    new_residual[...] = res_new[0:SIDES, :]
    new_direction[...] = (res_new + exact_dot(conj_t, dirs))[0:SIDES, :]

    for j in range(1, ROWS):
        gather_copy(j).wait_send()
        back_copy(j).wait_send()
    for k in range(1, COLS + 1):
        column_copy(k).wait_send()
        forward_copy(k).wait_send()


def on_device(points, lengthscale, noise, solution, residual, direction):
    scale = (math.sqrt(5.0) / LN2 / lengthscale)[:, None]
    vmem = pl.BlockSpec(memory_space=pltpu.VMEM)
    sem = pltpu.SemaphoreType.DMA
    rows = ROWS * PTS
    return pl.pallas_call(
        kernel,
        out_shape=[jax.ShapeDtypeStruct((SIDES, PTS), F32)] * 3,
        in_specs=[vmem] * 6,
        out_specs=[vmem] * 3,
        scratch_shapes=[
            pltpu.VMEM((PACKET, PTS), F32),
            pltpu.VMEM((ROWS, PACKET, PTS), F32),
            pltpu.VMEM((COLS + 1, PACKET, PTS), F32),
            pltpu.VMEM((rows, DEPTH), BF16),
            pltpu.VMEM((2 * SIDES_PAD, rows), BF16),
            pltpu.VMEM((LOW, rows), F32),
            pltpu.VMEM((LOW, rows), F8),
            pltpu.VMEM((LOW, LANES), F32),
            pltpu.VMEM((DEPTH, PTS), BF16),
            pltpu.VMEM((PTS, LANES), BF16),
            pltpu.VMEM((PTS, LANES), F8),
            pltpu.VMEM((8, LANES), F32),
            pltpu.VMEM((COLS + 1, 2 * SIDES_PAD, PTS), F32),
            pltpu.VMEM((rows, LANES), F32),
            pltpu.VMEM((COLS + 1, SIDES_PAD, PTS), F32),
            pltpu.VMEM((COLS + 1, SIDES_PAD, PTS), F32),
            pltpu.VMEM((ROWS, SIDES_PAD, PTS), F32),
            pltpu.VMEM((ROWS, SIDES_PAD, PTS), F32),
            pltpu.VMEM((SIDES_PAD, PTS), F32),
            pltpu.VMEM((SIDES_PAD, PTS), F32),
            pltpu.VMEM((SIDES_PAD, PTS), F32),
            pltpu.VMEM((SIDES_PAD, 128), F32),
            pltpu.VMEM((ROWS, SIDES_PAD, 128), F32),
            pltpu.VMEM((PLANE, SIDES_PAD, 128), F32),
            pltpu.VMEM((SIDES_PAD, PTS), F32),
            sem((ROWS,)), sem((ROWS,)), sem((COLS + 1,)), sem((COLS + 1,)),
            sem((COLS + 1,)), sem((COLS + 1,)), sem((ROWS,)), sem((ROWS,)),
            sem((ROWS,)), sem((ROWS,)), sem((PLANE,)), sem((PLANE,)),
        ],
        compiler_params=pltpu.CompilerParams(
            collective_id=0, has_side_effects=True, vmem_limit_bytes=56 * 2**20
        ),
        cost_estimate=pl.CostEstimate(flops=30_000_000_000, bytes_accessed=1_000_000, transcendentals=34_000_000),
        name="block_cg",
    )(points, scale, noise.reshape(1, 1), solution, residual, direction)


def solution(mesh):
    placed = P(None, ("blk", "narrow"))
    return jax.shard_map(
        on_device,
        mesh=mesh,
        in_specs=(placed, P(), P(), placed, placed, placed),
        out_specs=(placed, placed, placed),
        check_vma=False,
    )
```

time: 107 us -> 93.9 us (0.88)
  Pallas kernels: 101 us -> 88.1 us
    pallas_call x1, Pallas kernels: 101 us -> 88.1 us  [on_device(): pl.pallas_call(kernel, out_shape=[jax.ShapeDtypeStruct((SIDES, PTS), F32)...]
where the time goes in v2:
time: 93.9 us; the launch traced here: 93.6 us
  Pallas kernels  88.1 us (94%)
  local copies, waits for them, and re-layouts  4.22 us (4%)
  between operations  1.31 us (1%)
    pallas_call x1, Pallas kernels, on_device(): pl.pallas_call(kernel, out_shape=[jax.ShapeDtypeStruct((SIDES, PTS), F32)...  88.1 us
    unnamed x9, local copies, waits for them, and re-layouts  3.52 us

profile of v2, /device:TPU:1, one launch (start us, length us, event | category | flops | bytes accessed | tf_op | source)
XLA Modules:
  0.0 93.6 jit_solution(4354157552320004675)
XLA Ops:
  1.3 0.0 copy-start.2
  1.3 0.6 copy-done.2
  1.9 0.7 copy.9.scale
  2.6 88.1 %block_cg.1 = (f32[17,512]{1,0:T(8,128)}, f32[17,512]{1,0:T(8,128)}, f32[17,512]{1,0:T(8,128)}) custom-call(f32[32,512]{1,0:T(8,128)} %points.1, f32[32,1]{1,0:T(8,128)} %copy.9.scale, f32[1,1]{1,0:T(1,128)} %bitcast.3.noise, f32[17,512]{1,0:T(8,128)} %solution.1, f32[17,512]{1,0:T(8,128)} %residual.1, f32[17,512]{1,0:T(8,128)} %direction.1), custom_call_target="tpu_custom_call" | custom-call | flops 30000001024 | bytes 1000000 | tf_op jit(solution)/shard_map/block_cg/pallas_call | solution.py:347
  90.7 0.0 copy-start.1
  90.7 1.4 %copy.14 = f32[17,512]{1,0:T(8,128)} copy(f32[17,512]{1,0:T(8,128)} %get-tuple-element.6) | data formatting | bytes 69632
  92.2 0.0 copy-done.1
  92.2 0.0 copy-start
  92.2 0.6 copy.15
  92.8 0.2 copy-done
  93.0 0.6 copy.16
  (1 shorter events, 0.0 us)
Async XLA Ops:
  1.3 0.7 copy-start.2
  90.7 1.4 %copy-start.1 = (f32[17,512]{1,0:T(8,128)S(1)}, f32[17,512]{1,0:T(8,128)}, u32[]{:S(2)}) copy-start(f32[17,512]{1,0:T(8,128)} %get-tuple-element.7) | copy-start | bytes 104452
  92.2 0.8 copy-start

commit v3 on v2

--- a/solution.py
+++ b/solution.py
@@ -24,11 +24,11 @@
 COLS = len(OFFSETS)
 STEP_X = tuple(dx for dx, _ in OFFSETS)
 STEP_Z = tuple(dz for _, dz in OFFSETS)
-PACKET = 56
+PACKET = 49
 DEPTH = 256
 CHUNK = 2048
 LANES = 128
-LOW = 32
+LOW = 64
 BOOST = 14
 F8 = jnp.float8_e4m3fn
 F8_TOP = 256.0
@@ -95,8 +95,8 @@
 
 
 def kernel(points, scale, noise, solution, residual, direction, new_solution, new_residual, new_direction,
-           pkt, gat, cols, left, ldir, ldirf, ldir8, lscale, right, rdir, rdir8, rscale, fwds, back, rsend, rrecv, bsend, brecv, dir24, res24, img24,
-           gram, ar1, ar2, own,
+           pkt, gat, cols, left, ldir, ldirf, ldir8, lscale, right, rdir, rdir8, rscale, side24, fwds, back, rsend, rrecv, bsend, brecv, dir24, res24, img24,
+           gram, ar1, ar2, own, tot24,
            gat_send, gat_recv, col_send, col_recv, r_send, r_recv, b_send, b_recv,
            ar1_send, ar1_recv, ar2_send, ar2_recv):
     b = lax.axis_index("blk")
@@ -128,7 +128,8 @@
     res24[...] = jnp.zeros_like(res24)
     res24[0:SIDES, :] = residual[...]
     pkt[0:FEATS, :] = points[...] * scale[...]
-    pkt[FEATS:PACKET, :] = dir24[...]
+    pkt[FEATS:PACKET, :] = direction[...]
+    side24[...] = jnp.zeros_like(side24)
     pl.semaphore_wait(barrier, ROWS + PLANE - 2)
 
     def gather_copy(j):
@@ -152,73 +153,82 @@
             device_id=row_peer(j), device_id_type=MESH)
 
     middle = ROWS // 2
-    for j in range(1, middle + 1):
+    for j in range(1, middle):
         gather_copy(j).start()
     for k in range(1, COLS + 1):
         column_copy(k).start()
 
-    def load_right(packet):
-        right[...] = expand(packet[0:FEATS, :], False).astype(BF16)
-        rows = packet[FEATS:PACKET, :]
+    def padded_sides(packet):
+        side24[0:SIDES, :] = packet[FEATS:PACKET, :]
+        return side24[...]
+
+    def low_terms(rows, top):
+        scaled = rows * (F8_TOP / top)
+        first = scaled.astype(F8).astype(F32)
+        return first, scaled - first
+
+    def load_right(k, packet):
+        right[k] = expand(packet[0:FEATS, :], False).astype(BF16)
+        rows = padded_sides(packet)
         hi = rows.astype(BF16).astype(F32)
-        spare = jnp.zeros((LANES - 2 * SIDES_PAD, PTS), F32)
-        rdir[...] = jnp.concatenate([hi, rows - hi, spare], 0).T.astype(BF16)
-        plain = jnp.concatenate([rows, jnp.zeros((LANES - SIDES_PAD, PTS), F32)], 0).T
-        top = jnp.maximum(jnp.max(jnp.abs(plain), 0, keepdims=True), 1e-30)
-        rdir8[...] = (plain * (F8_TOP / top)).astype(F8)
-        rscale[...] = jnp.broadcast_to(top * (1.0 / F8_TOP), (8, LANES))
-
-    def scale_left(at):
+        top = jnp.maximum(jnp.max(jnp.abs(rows), 1, keepdims=True), 1e-30)
+        first, second = low_terms(rows, top)
+        scale_rows = jnp.broadcast_to(top * (1.0 / F8_TOP), rows.shape)
+        spare = jnp.zeros((LANES - 5 * SIDES_PAD, PTS), F32)
+        turned = jnp.concatenate([hi, rows - hi, first, second, scale_rows, spare], 0).T
+        lane = lax.broadcasted_iota(jnp.int32, (PTS, LANES), 1)
+        rdir[k] = jnp.where(lane < 2 * SIDES_PAD, turned, 0.0).astype(BF16)
+        low = (lane >= 2 * SIDES_PAD) & (lane < 4 * SIDES_PAD)
+        rdir8[k] = jnp.where(low, turned, 0.0).astype(F8)
+        line = turned[0:8, :]
+        near = pltpu.roll(line, LANES - SIDES_PAD, 1)
+        far = pltpu.roll(line, LANES - 2 * SIDES_PAD, 1)
+        rscale[k] = jnp.where(lane[0:8, :] < 3 * SIDES_PAD, far, near)
+
+    def scale_left(half, at):
         rows = ldirf[:, at]
         top = jnp.maximum(jnp.max(jnp.abs(rows), 1, keepdims=True), 1e-30)
-        ldir8[:, at] = (rows * (F8_TOP / top)).astype(F8)
-        lscale[...] = jnp.broadcast_to(top * (1.0 / F8_TOP), (LOW, LANES))
+        first, second = low_terms(rows, top)
+        spare = jnp.zeros((LOW - 2 * SIDES_PAD, rows.shape[1]), F32)
+        ldir8[:, at] = jnp.concatenate([first, second, spare], 0).astype(F8)
+        lscale[half] = jnp.broadcast_to(top * (1.0 / F8_TOP), (SIDES_PAD, LANES))
 
     def load_left(j, packet):
         at = pl.ds(pl.multiple_of(j * PTS, PTS), PTS)
         left[at, :] = expand(packet[0:FEATS, :], True).T.astype(BF16)
-        rows = packet[FEATS:PACKET, :]
+        rows = padded_sides(packet)
         ldir[:, at] = split_dir(rows)
-        ldirf[:, at] = jnp.concatenate([rows, jnp.zeros((LOW - SIDES_PAD, PTS), F32)], 0)
-        return at
-
-    def tile(k, start, size):
-        at = pl.ds(pl.multiple_of(start, PTS), size)
-        kern = matern(dot(left[at, :], right[...]))
+        ldirf[:, at] = rows
+
+    def tile(k, start, half, both):
+        at = pl.ds(pl.multiple_of(start, PTS), CHUNK)
+        kern = matern(dot(left[at, :], right[k]))
         hi = kern.astype(BF16)
         lo = (kern - hi.astype(F32)).astype(F8)
-        back[at, :] += dot(hi, rdir[...])
-        back[at, :] += dot(lo, rdir8[...]) * rscale[0:1, :]
+        if both:
+            back[at, :] += dot(hi, rdir[k])
+            back[at, :] += dot(lo, rdir8[k]) * rscale[k, 0:1]
         fwds[k] += dot(ldir[:, at], hi)
-        fwds[k, 0:LOW] += dot(ldir8[:, at], lo) * lscale[:, 0:1]
+        low = dot(ldir8[:, at], lo)
+        fwds[k, 0:SIDES_PAD] += (low[0:SIDES_PAD] + low[SIDES_PAD:2 * SIDES_PAD]) * lscale[half, :, 0:1]
 
     back[...] = jnp.zeros_like(back)
     fwds[...] = jnp.zeros_like(fwds)
-    load_right(pkt)
-
-    @pl.loop(0, middle + 1)
+    right[0] = expand(pkt[0:FEATS, :], False).astype(BF16)
+    load_left(0, pkt)
+
+    @pl.loop(1, middle)
     def _(j):
-        @pl.when(j > 0)
-        def _():
-            gather_copy(j).wait_recv()
-
-        @pl.when(j == 0)
-        def _():
-            gat[0] = pkt[...]
-
-        scale_left(load_left(j, gat.at[j]))
-        tile(0, j * PTS, PTS)
-
-    own[...] = fwds[0, 0:SIDES_PAD] + fwds[0, SIDES_PAD:]
-    back[0:PTS, :] = jnp.zeros((PTS, LANES), F32)
-    back[middle * PTS:(middle + 1) * PTS, :] = jnp.zeros((PTS, LANES), F32)
-    scale_left(pl.ds(0, (middle + 1) * PTS))
+        gather_copy(j).wait_recv()
+        load_left(j, gat.at[j])
+
+    scale_left(0, pl.ds(0, middle * PTS))
     upper_x = jnp.where(x >= SIDE // 2, PTS, 0)
     upper_z = jnp.where(z >= SIDE // 2, PTS, 0)
 
     def back_slice(j):
         part = back[pl.ds(pl.multiple_of(j * PTS, PTS), PTS), :].T
-        return part[0:SIDES_PAD, :] + part[SIDES_PAD:2 * SIDES_PAD, :]
+        return sum(part[i * SIDES_PAD:i * SIDES_PAD + SIDES, :] for i in range(4))
 
     def send_back(first, last):
         @pl.loop(first, last)
@@ -234,10 +244,17 @@
         @pl.when(first)
         def _():
             column_copy(k).wait_recv()
-
-        @pl.when((s >= 1) & (s < ROWS - middle))
+            load_right(k, cols.at[k])
+
+        @pl.when(s < ROWS - middle)
         def _():
             gather_copy(s + middle).start()
+
+        @pl.when(s == FULL)
+        def _():
+            gather_copy(middle).wait_recv()
+            load_left(middle, gat.at[middle])
+            scale_left(0, pl.ds(0, (middle + 1) * PTS))
 
         @pl.when(s == COLS)
         def _():
@@ -246,27 +263,31 @@
                 gather_copy(j).wait_recv()
                 load_left(j, gat.at[j])
 
-            scale_left(pl.ds(middle * PTS, (ROWS - middle) * PTS))
+            scale_left(1, pl.ds(middle * PTS, (ROWS - middle) * PTS))
             send_back(1, middle)
 
-        load_right(cols.at[k])
         upper = jnp.where(k == FULL + 2, upper_z, upper_x)
-        tile(k, jnp.where(first, jnp.where(k > FULL, upper, 0), CHUNK), CHUNK)
+        tile(k, jnp.where(first, jnp.where(k > FULL, upper, 0), CHUNK), jnp.where(first, 0, 1), True)
 
         @pl.when(s >= FULL)
         def _():
-            rsend[k] = fwds[k, 0:SIDES_PAD] + fwds[k, SIDES_PAD:]
+            rsend[k] = fwds[k, 0:SIDES] + fwds[k, SIDES_PAD:SIDES_PAD + SIDES]
             forward_copy(k).start()
 
     send_back(middle, ROWS)
 
-    own[...] += back_slice(0)
+    @pl.loop(0, 2)
+    def _(half):
+        tile(0, half * CHUNK, half, False)
+
+    own[...] = fwds[0, 0:SIDES_PAD] + fwds[0, SIDES_PAD:]
+    own[0:SIDES, :] += back_slice(0)
     for k in range(1, COLS + 1):
         forward_copy(k).wait_recv()
-        own[...] += rrecv[k]
+        own[0:SIDES, :] += rrecv[k]
     for j in range(1, ROWS):
         back_copy(j).wait_recv()
-        own[...] += brecv[j]
+        own[0:SIDES, :] += brecv[j]
     img24[...] = own[...] * (LN2 * LN2 / 3.0 / 2.0**BOOST) + noise[...] * dir24[...]
 
     zeros8 = jnp.zeros((8, PTS), F32)
@@ -274,7 +295,7 @@
     img, dirs, res = img24[...], dir24[...], res24[...]
     table = jnp.concatenate([dirs, zeros8, img, zeros8, zeros64], 0)
     other = jnp.concatenate([zeros64, img, zeros8, dirs, zeros8], 0)
-    gram[...] = exact_dot(img, table, ((1,), (1,))) + exact_dot(res, other, ((1,), (1,)))
+    gram[...] = (exact_dot(img, table, ((1,), (1,))) + exact_dot(res, other, ((1,), (1,))))[0:SIDES, :]
 
     def ar1_copy(j):
         return pltpu.make_async_remote_copy(
@@ -308,6 +329,9 @@
     for k in range(1, PLANE):
         total = total + ar2[k]
 
+    tot24[...] = jnp.zeros_like(tot24)
+    tot24[0:SIDES, :] = total
+    total = tot24[...]
     curv = total[:, 0:SIDES_PAD]
     curv = 0.5 * (curv + curv.T)
     outer = pltpu.roll(total, 96, 1)[:, 0:SIDES_PAD]
@@ -355,26 +379,28 @@
             pltpu.VMEM((COLS + 1, PACKET, PTS), F32),
             pltpu.VMEM((rows, DEPTH), BF16),
             pltpu.VMEM((2 * SIDES_PAD, rows), BF16),
-            pltpu.VMEM((LOW, rows), F32),
+            pltpu.VMEM((SIDES_PAD, rows), F32),
             pltpu.VMEM((LOW, rows), F8),
-            pltpu.VMEM((LOW, LANES), F32),
-            pltpu.VMEM((DEPTH, PTS), BF16),
-            pltpu.VMEM((PTS, LANES), BF16),
-            pltpu.VMEM((PTS, LANES), F8),
-            pltpu.VMEM((8, LANES), F32),
+            pltpu.VMEM((2, SIDES_PAD, LANES), F32),
+            pltpu.VMEM((COLS + 1, DEPTH, PTS), BF16),
+            pltpu.VMEM((COLS + 1, PTS, LANES), BF16),
+            pltpu.VMEM((COLS + 1, PTS, LANES), F8),
+            pltpu.VMEM((COLS + 1, 8, LANES), F32),
+            pltpu.VMEM((SIDES_PAD, PTS), F32),
             pltpu.VMEM((COLS + 1, 2 * SIDES_PAD, PTS), F32),
             pltpu.VMEM((rows, LANES), F32),
-            pltpu.VMEM((COLS + 1, SIDES_PAD, PTS), F32),
-            pltpu.VMEM((COLS + 1, SIDES_PAD, PTS), F32),
-            pltpu.VMEM((ROWS, SIDES_PAD, PTS), F32),
-            pltpu.VMEM((ROWS, SIDES_PAD, PTS), F32),
+            pltpu.VMEM((COLS + 1, SIDES, PTS), F32),
+            pltpu.VMEM((COLS + 1, SIDES, PTS), F32),
+            pltpu.VMEM((ROWS, SIDES, PTS), F32),
+            pltpu.VMEM((ROWS, SIDES, PTS), F32),
             pltpu.VMEM((SIDES_PAD, PTS), F32),
             pltpu.VMEM((SIDES_PAD, PTS), F32),
             pltpu.VMEM((SIDES_PAD, PTS), F32),
-            pltpu.VMEM((SIDES_PAD, 128), F32),
-            pltpu.VMEM((ROWS, SIDES_PAD, 128), F32),
-            pltpu.VMEM((PLANE, SIDES_PAD, 128), F32),
+            pltpu.VMEM((SIDES, LANES), F32),
+            pltpu.VMEM((ROWS, SIDES, LANES), F32),
+            pltpu.VMEM((PLANE, SIDES, LANES), F32),
             pltpu.VMEM((SIDES_PAD, PTS), F32),
+            pltpu.VMEM((SIDES_PAD, LANES), F32),
             sem((ROWS,)), sem((ROWS,)), sem((COLS + 1,)), sem((COLS + 1,)),
             sem((COLS + 1,)), sem((COLS + 1,)), sem((ROWS,)), sem((ROWS,)),
             sem((ROWS,)), sem((ROWS,)), sem((PLANE,)), sem((PLANE,)),

time: 93.9 us -> 87.6 us (0.933)
  Pallas kernels: 88.1 us -> 81.7 us
    pallas_call x1, Pallas kernels: 88.1 us -> 81.7 us  [on_device(): pl.pallas_call(kernel, out_shape=[jax.ShapeDtypeStruct((SIDES, PTS), F32)...]
where the time goes in v3:
time: 87.6 us; the launch traced here: 87.3 us
  Pallas kernels  81.7 us (93%)
  local copies, waits for them, and re-layouts  4.22 us (5%)
  between operations  1.31 us (1%)
    pallas_call x1, Pallas kernels, on_device(): pl.pallas_call(kernel, out_shape=[jax.ShapeDtypeStruct((SIDES, PTS), F32)...  81.7 us
    unnamed x9, local copies, waits for them, and re-layouts  3.52 us

profile of v3, /device:TPU:1, one launch (start us, length us, event | category | flops | bytes accessed | tf_op | source)
XLA Modules:
  0.0 87.3 jit_solution(1974744891292838805)
XLA Ops:
  1.3 0.0 copy-start.2
  1.3 0.6 copy-done.2
  1.9 0.7 copy.9.scale
  2.6 81.7 %block_cg.1 = (f32[17,512]{1,0:T(8,128)}, f32[17,512]{1,0:T(8,128)}, f32[17,512]{1,0:T(8,128)}) custom-call(f32[32,512]{1,0:T(8,128)} %points.1, f32[32,1]{1,0:T(8,128)} %copy.9.scale, f32[1,1]{1,0:T(1,128)} %bitcast.3.noise, f32[17,512]{1,0:T(8,128)} %solution.1, f32[17,512]{1,0:T(8,128)} %residual.1, f32[17,512]{1,0:T(8,128)} %direction.1), custom_call_target="tpu_custom_call" | custom-call | flops 30000001024 | bytes 1000000 | tf_op jit(solution)/shard_map/block_cg/pallas_call | solution.py:371
  84.4 0.0 copy-start.1
  84.4 1.4 %copy.14 = f32[17,512]{1,0:T(8,128)} copy(f32[17,512]{1,0:T(8,128)} %get-tuple-element.6) | data formatting | bytes 69632
  85.8 0.0 copy-done.1
  85.8 0.0 copy-start
  85.8 0.6 copy.15
  86.5 0.2 copy-done
  86.7 0.6 copy.16
  (1 shorter events, 0.0 us)
Async XLA Ops:
  1.3 0.7 copy-start.2
  84.4 1.4 %copy-start.1 = (f32[17,512]{1,0:T(8,128)S(1)}, f32[17,512]{1,0:T(8,128)}, u32[]{:S(2)}) copy-start(f32[17,512]{1,0:T(8,128)} %get-tuple-element.7) | copy-start | bytes 104452
  85.8 0.8 copy-start

commit v4 on v3

--- a/solution.py
+++ b/solution.py
@@ -22,6 +22,9 @@
 FULL = 6
 OFFSETS = ((1, 0), (0, 3), (1, 1), (3, 1), (2, 3), (3, 2), (2, 0), (0, 2), (2, 2))
 COLS = len(OFFSETS)
+ROW_OFFSETS = ((0, 0), (0, 1), (1, 0), (3, 1), (2, 0), (2, 1), (1, 1), (3, 0))
+ROW_Y = tuple(dy for dy, _ in ROW_OFFSETS[1:])
+ROW_C = tuple(dc for _, dc in ROW_OFFSETS[1:])
 STEP_X = tuple(dx for dx, _ in OFFSETS)
 STEP_Z = tuple(dz for _, dz in OFFSETS)
 PACKET = 49
@@ -94,9 +97,9 @@
     return out
 
 
-def kernel(points, scale, noise, solution, residual, direction, new_solution, new_residual, new_direction,
-           pkt, gat, cols, left, ldir, ldirf, ldir8, lscale, right, rdir, rdir8, rscale, side24, fwds, back, rsend, rrecv, bsend, brecv, dir24, res24, img24,
-           gram, ar1, ar2, own, tot24,
+def kernel(points, scale, noise, residual, direction, img24, total_out,
+           pkt, gat, cols, left, ldir, ldirf, ldir8, lscale, right, rdir, rdir8, rscale, side24, fwds, back, rsend, rrecv, bsend, brecv, dir24, res24,
+           gram, ar1, ar2, own,
            gat_send, gat_recv, col_send, col_recv, r_send, r_recv, b_send, b_recv,
            ar1_send, ar1_recv, ar2_send, ar2_recv):
     b = lax.axis_index("blk")
@@ -104,22 +107,24 @@
 
     x = b // 8 * 2 + n % 2
     z = b // 2 % SIDE
-    m = n // 2 * 2 + b % 2
-
-    def device(x, z, m):
-        return (x // 2 * 8 + z * 2 + m % 2, m // 2 * 2 + x % 2)
-
-    def row_peer(j):
-        return device(x, z, lax.rem(m + j, ROWS))
+    y = n // 2
+    c = b % 2
+    m = y * 2 + c
+
+    def device(x, z, y, c):
+        return (x // 2 * 8 + z * 2 + c, y * 2 + x % 2)
+
+    def row_peer(dy, dc):
+        return device(x, z, lax.rem(y + dy, SIDE), lax.rem(c + dc, 2))
 
     def plane_peer(dx, dz):
-        return device(lax.rem(x + dx, SIDE), lax.rem(z + dz, SIDE), m)
+        return device(lax.rem(x + dx, SIDE), lax.rem(z + dz, SIDE), y, c)
 
     others = [(dx, dz) for dx in range(SIDE) for dz in range(SIDE) if dx or dz]
 
     barrier = pltpu.get_barrier_semaphore()
     for j in range(1, ROWS):
-        pl.semaphore_signal(barrier, inc=1, device_id=row_peer(j), device_id_type=MESH)
+        pl.semaphore_signal(barrier, inc=1, device_id=row_peer(pick(j, ROW_Y), pick(j, ROW_C)), device_id_type=MESH)
     for dx, dz in others:
         pl.semaphore_signal(barrier, inc=1, device_id=plane_peer(dx, dz), device_id_type=MESH)
 
@@ -135,7 +140,7 @@
     def gather_copy(j):
         return pltpu.make_async_remote_copy(
             src_ref=pkt, dst_ref=gat.at[j], send_sem=gat_send.at[j], recv_sem=gat_recv.at[j],
-            device_id=row_peer(ROWS - j), device_id_type=MESH)
+            device_id=row_peer(SIDE - pick(j, ROW_Y), pick(j, ROW_C)), device_id_type=MESH)
 
     def column_copy(k):
         return pltpu.make_async_remote_copy(
@@ -150,7 +155,7 @@
     def back_copy(j):
         return pltpu.make_async_remote_copy(
             src_ref=bsend.at[j], dst_ref=brecv.at[j], send_sem=b_send.at[j], recv_sem=b_recv.at[j],
-            device_id=row_peer(j), device_id_type=MESH)
+            device_id=row_peer(pick(j, ROW_Y), pick(j, ROW_C)), device_id_type=MESH)
 
     middle = ROWS // 2
     for j in range(1, middle):
@@ -223,8 +228,8 @@
         load_left(j, gat.at[j])
 
     scale_left(0, pl.ds(0, middle * PTS))
-    upper_x = jnp.where(x >= SIDE // 2, PTS, 0)
-    upper_z = jnp.where(z >= SIDE // 2, PTS, 0)
+    upper_x = jnp.where(x >= SIDE // 2, 2 * PTS, 0)
+    upper_z = jnp.where(z >= SIDE // 2, 2 * PTS, 0)
 
     def back_slice(j):
         part = back[pl.ds(pl.multiple_of(j * PTS, PTS), PTS), :].T
@@ -252,13 +257,16 @@
 
         @pl.when(s == FULL)
         def _():
-            gather_copy(middle).wait_recv()
-            load_left(middle, gat.at[middle])
-            scale_left(0, pl.ds(0, (middle + 1) * PTS))
+            @pl.loop(middle, middle + 2)
+            def _(j):
+                gather_copy(j).wait_recv()
+                load_left(j, gat.at[j])
+
+            scale_left(0, pl.ds(0, (middle + 2) * PTS))
 
         @pl.when(s == COLS)
         def _():
-            @pl.loop(middle + 1, ROWS)
+            @pl.loop(middle + 2, ROWS)
             def _(j):
                 gather_copy(j).wait_recv()
                 load_left(j, gat.at[j])
@@ -300,7 +308,7 @@
     def ar1_copy(j):
         return pltpu.make_async_remote_copy(
             src_ref=gram, dst_ref=ar1.at[m], send_sem=ar1_send.at[j], recv_sem=ar1_recv.at[j],
-            device_id=row_peer(j), device_id_type=MESH)
+            device_id=row_peer(pick(j, ROW_Y), pick(j, ROW_C)), device_id_type=MESH)
 
     for j in range(1, ROWS):
         ar1_copy(j).start()
@@ -329,9 +337,23 @@
     for k in range(1, PLANE):
         total = total + ar2[k]
 
-    tot24[...] = jnp.zeros_like(tot24)
-    tot24[0:SIDES, :] = total
-    total = tot24[...]
+    total_out[...] = jnp.zeros_like(total_out)
+    total_out[0:SIDES, :] = total
+
+    for j in range(1, ROWS):
+        gather_copy(j).wait_send()
+        back_copy(j).wait_send()
+    for k in range(1, COLS + 1):
+        column_copy(k).wait_send()
+        forward_copy(k).wait_send()
+
+
+def solve_kernel(img24, total_in, solution, residual, direction, new_solution, new_residual, new_direction, dir24):
+    total = total_in[...]
+    img = img24[...]
+    dir24[...] = jnp.zeros_like(dir24)
+    dir24[0:SIDES, :] = direction[...]
+    dirs = dir24[...]
     curv = total[:, 0:SIDES_PAD]
     curv = 0.5 * (curv + curv.T)
     outer = pltpu.roll(total, 96, 1)[:, 0:SIDES_PAD]
@@ -350,17 +372,11 @@
 
     step_t = exact_dot(dir_res, inverse)
     conj_t = exact_dot(exact_dot(step_t, outer) - img_res, inverse)
-    res_new = res - exact_dot(step_t, img)
+    moved = exact_dot(step_t, img)
     new_solution[...] = solution[...] + exact_dot(step_t, dirs)[0:SIDES, :]
-    new_residual[...] = res_new[0:SIDES, :]
-    new_direction[...] = (res_new + exact_dot(conj_t, dirs))[0:SIDES, :]
-
-    for j in range(1, ROWS):
-        gather_copy(j).wait_send()
-        back_copy(j).wait_send()
-    for k in range(1, COLS + 1):
-        column_copy(k).wait_send()
-        forward_copy(k).wait_send()
+    res_new = residual[...] - moved[0:SIDES, :]
+    new_residual[...] = res_new
+    new_direction[...] = res_new + exact_dot(conj_t, dirs)[0:SIDES, :]
 
 
 def on_device(points, lengthscale, noise, solution, residual, direction):
@@ -368,11 +384,11 @@
     vmem = pl.BlockSpec(memory_space=pltpu.VMEM)
     sem = pltpu.SemaphoreType.DMA
     rows = ROWS * PTS
-    return pl.pallas_call(
+    image, total = pl.pallas_call(
         kernel,
-        out_shape=[jax.ShapeDtypeStruct((SIDES, PTS), F32)] * 3,
-        in_specs=[vmem] * 6,
-        out_specs=[vmem] * 3,
+        out_shape=[jax.ShapeDtypeStruct((SIDES_PAD, PTS), F32), jax.ShapeDtypeStruct((SIDES_PAD, LANES), F32)],
+        in_specs=[vmem] * 5,
+        out_specs=[vmem] * 2,
         scratch_shapes=[
             pltpu.VMEM((PACKET, PTS), F32),
             pltpu.VMEM((ROWS, PACKET, PTS), F32),
@@ -395,12 +411,10 @@
             pltpu.VMEM((ROWS, SIDES, PTS), F32),
             pltpu.VMEM((SIDES_PAD, PTS), F32),
             pltpu.VMEM((SIDES_PAD, PTS), F32),
-            pltpu.VMEM((SIDES_PAD, PTS), F32),
             pltpu.VMEM((SIDES, LANES), F32),
             pltpu.VMEM((ROWS, SIDES, LANES), F32),
             pltpu.VMEM((PLANE, SIDES, LANES), F32),
             pltpu.VMEM((SIDES_PAD, PTS), F32),
-            pltpu.VMEM((SIDES_PAD, LANES), F32),
             sem((ROWS,)), sem((ROWS,)), sem((COLS + 1,)), sem((COLS + 1,)),
             sem((COLS + 1,)), sem((COLS + 1,)), sem((ROWS,)), sem((ROWS,)),
             sem((ROWS,)), sem((ROWS,)), sem((PLANE,)), sem((PLANE,)),
@@ -410,7 +424,15 @@
         ),
         cost_estimate=pl.CostEstimate(flops=30_000_000_000, bytes_accessed=1_000_000, transcendentals=34_000_000),
         name="block_cg",
-    )(points, scale, noise.reshape(1, 1), solution, residual, direction)
+    )(points, scale, noise.reshape(1, 1), residual, direction)
+    return pl.pallas_call(
+        solve_kernel,
+        out_shape=[jax.ShapeDtypeStruct((SIDES, PTS), F32)] * 3,
+        in_specs=[vmem] * 5,
+        out_specs=[vmem] * 3,
+        scratch_shapes=[pltpu.VMEM((SIDES_PAD, PTS), F32)],
+        name="solve",
+    )(image, total, solution, residual, direction)
 
 
 def solution(mesh):

time: 87.6 us -> 84.6 us (0.966)
  local copies, waits for them, and re-layouts: 4.22 us -> 1.35 us
    unnamed x9 -> x2, local copies, waits for them, and re-layouts: 3.52 us -> 0.65 us
    pallas_call x1 -> x2, Pallas kernels: 81.7 us -> 81.7 us  [the longest x1 78.1 us: on_device(): pl.pallas_call(kernel, out_shape=[jax.ShapeDtypeStruct((SIDES_PAD, PTS),...]
where the time goes in v4:
time: 84.6 us; the launch traced here: 84.4 us
  Pallas kernels  81.7 us (97%)
  local copies, waits for them, and re-layouts  1.35 us (2%)
  between operations  1.29 us (2%)
    pallas_call x1, Pallas kernels, on_device(): pl.pallas_call(kernel, out_shape=[jax.ShapeDtypeStruct((SIDES_PAD, PTS),...  78.1 us
    pallas_call x1, Pallas kernels, on_device(): pl.pallas_call(solve_kernel, out_shape=[jax.ShapeDtypeStruct((SIDES, PTS)...  3.61 us

profile of v4, /device:TPU:1, one launch (start us, length us, event | category | flops | bytes accessed | tf_op | source)
XLA Modules:
  0.0 84.4 jit_solution(720063936980152380)
XLA Ops:
  1.3 0.0 copy-start
  1.3 0.6 copy-done
  1.9 0.7 copy.9.scale
  2.6 78.1 %block_cg.1 = (f32[24,512]{1,0:T(8,128)}, f32[24,128]{1,0:T(8,128)}) custom-call(f32[32,512]{1,0:T(8,128)} %points.1, f32[32,1]{1,0:T(8,128)} %copy.9.scale, f32[1,1]{1,0:T(1,128)} %bitcast.3.noise, f32[17,512]{1,0:T(8,128)} %residual.3, f32[17,512]{1,0:T(8,128)} %direction.3), custom_call_target="tpu_custom_call" | custom-call | flops 30000001024 | bytes 1000000 | tf_op jit(solution)/shard_map/block_cg/pallas_call | solution.py:387
  80.8 3.6 %solve.1 = (f32[17,512]{1,0:T(8,128)}, f32[17,512]{1,0:T(8,128)}, f32[17,512]{1,0:T(8,128)}) custom-call(f32[24,512]{1,0:T(8,128)} %get-tuple-element.5.img24, f32[24,128]{1,0:T(8,128)} %get-tuple-element.6.total_in, f32[17,512]{1,0:T(8,128)} %solution.1, f32[17,512]{1,0:T(8,128)} %residual.3, f32[17,512]{1,0:T(8,128)} %direction.3), custom_call_target="tpu_custom_call" | custom-call | tf_op jit(solution)/shard_map/solve/pallas_call | solution.py:428
  (1 shorter events, 0.0 us)
Async XLA Ops:
  1.3 0.7 copy-start

commit v5 on v4

--- a/solution.py
+++ b/solution.py
@@ -97,7 +97,7 @@
     return out
 
 
-def kernel(points, scale, noise, residual, direction, img24, total_out,
+def kernel(points, lengthscale, noise, residual, direction, img24, total_out,
            pkt, gat, cols, left, ldir, ldirf, ldir8, lscale, right, rdir, rdir8, rscale, side24, fwds, back, rsend, rrecv, bsend, brecv, dir24, res24,
            gram, ar1, ar2, own,
            gat_send, gat_recv, col_send, col_recv, r_send, r_recv, b_send, b_recv,
@@ -132,7 +132,9 @@
     dir24[0:SIDES, :] = direction[...]
     res24[...] = jnp.zeros_like(res24)
     res24[0:SIDES, :] = residual[...]
-    pkt[0:FEATS, :] = points[...] * scale[...]
+    diagonal = lax.broadcasted_iota(jnp.int32, (FEATS, FEATS), 0) == lax.broadcasted_iota(jnp.int32, (FEATS, FEATS), 1)
+    lengths = jnp.sum(jnp.where(diagonal, jnp.broadcast_to(lengthscale[...], (FEATS, FEATS)), 0.0), 1, keepdims=True)
+    pkt[0:FEATS, :] = points[...] * (math.sqrt(5.0) / LN2 / lengths)
     pkt[FEATS:PACKET, :] = direction[...]
     side24[...] = jnp.zeros_like(side24)
     pl.semaphore_wait(barrier, ROWS + PLANE - 2)
@@ -207,15 +209,24 @@
 
     def tile(k, start, half, both):
         at = pl.ds(pl.multiple_of(start, PTS), CHUNK)
-        kern = matern(dot(left[at, :], right[k]))
-        hi = kern.astype(BF16)
-        lo = (kern - hi.astype(F32)).astype(F8)
-        if both:
-            back[at, :] += dot(hi, rdir[k])
-            back[at, :] += dot(lo, rdir8[k]) * rscale[k, 0:1]
-        fwds[k] += dot(ldir[:, at], hi)
-        low = dot(ldir8[:, at], lo)
-        fwds[k, 0:SIDES_PAD] += (low[0:SIDES_PAD] + low[SIDES_PAD:2 * SIDES_PAD]) * lscale[half, :, 0:1]
+        piece = 512
+        waiting = None
+        for place in range(0, CHUNK + piece, piece):
+            fresh = None
+            if place < CHUNK:
+                at = pl.ds(pl.multiple_of(start + place, PTS), piece)
+                kern = matern(dot(left[at, :], right[k]))
+                hi = kern.astype(BF16)
+                fresh = at, hi, (kern - hi.astype(F32)).astype(F8)
+            if waiting is not None:
+                at, hi, lo = waiting
+                if both:
+                    back[at, :] += dot(hi, rdir[k])
+                    back[at, :] += dot(lo, rdir8[k]) * rscale[k, 0:1]
+                fwds[k] += dot(ldir[:, at], hi)
+                low = dot(ldir8[:, at], lo)
+                fwds[k, 0:SIDES_PAD] += (low[0:SIDES_PAD] + low[SIDES_PAD:2 * SIDES_PAD]) * lscale[half, :, 0:1]
+            waiting = fresh
 
     back[...] = jnp.zeros_like(back)
     fwds[...] = jnp.zeros_like(fwds)
@@ -348,7 +359,7 @@
         forward_copy(k).wait_send()
 
 
-def solve_kernel(img24, total_in, solution, residual, direction, new_solution, new_residual, new_direction, dir24):
+def solve_kernel(img24, total_in, solution, residual, direction, new_solution, new_residual, new_direction, dir24, both):
     total = total_in[...]
     img = img24[...]
     dir24[...] = jnp.zeros_like(dir24)
@@ -359,16 +370,16 @@
     outer = pltpu.roll(total, 96, 1)[:, 0:SIDES_PAD]
     img_res = pltpu.roll(total, 64, 1)[:, 0:SIDES_PAD]
     dir_res = pltpu.roll(total, 32, 1)[:, 0:SIDES_PAD]
-    row = lax.broadcasted_iota(jnp.int32, (SIDES_PAD, SIDES_PAD), 0)
-    col = lax.broadcasted_iota(jnp.int32, (SIDES_PAD, SIDES_PAD), 1)
-    inverse = (row == col).astype(F32)
+    row = lax.broadcasted_iota(jnp.int32, (SIDES_PAD, LANES), 0)
+    col = lax.broadcasted_iota(jnp.int32, (SIDES_PAD, LANES), 1)
+    both[...] = (col == row + 32).astype(F32)
+    both[:, 0:SIDES_PAD] = curv
+    work = both[...]
     for i in range(SIDES):
-        pivot = 1.0 / curv[i:i + 1, i:i + 1]
-        head = curv[i:i + 1, :] * pivot
-        tail = inverse[i:i + 1, :] * pivot
-        factor = jnp.where(row[:, 0:1] == i, 0.0, curv[:, i:i + 1])
-        curv = jnp.where(row == i, head, curv - factor * head)
-        inverse = jnp.where(row == i, tail, inverse - factor * tail)
+        head = work[i:i + 1, :] * (1.0 / work[i:i + 1, i:i + 1])
+        factor = work[:, i:i + 1]
+        work = jnp.where(row == i, head, work - factor * head)
+    inverse = pltpu.roll(work, 96, 1)[:, 0:SIDES_PAD]
 
     step_t = exact_dot(dir_res, inverse)
     conj_t = exact_dot(exact_dot(step_t, outer) - img_res, inverse)
@@ -380,7 +391,6 @@
 
 
 def on_device(points, lengthscale, noise, solution, residual, direction):
-    scale = (math.sqrt(5.0) / LN2 / lengthscale)[:, None]
     vmem = pl.BlockSpec(memory_space=pltpu.VMEM)
     sem = pltpu.SemaphoreType.DMA
     rows = ROWS * PTS
@@ -424,13 +434,13 @@
         ),
         cost_estimate=pl.CostEstimate(flops=30_000_000_000, bytes_accessed=1_000_000, transcendentals=34_000_000),
         name="block_cg",
-    )(points, scale, noise.reshape(1, 1), residual, direction)
+    )(points, lengthscale.reshape(1, FEATS), noise.reshape(1, 1), residual, direction)
     return pl.pallas_call(
         solve_kernel,
         out_shape=[jax.ShapeDtypeStruct((SIDES, PTS), F32)] * 3,
         in_specs=[vmem] * 5,
         out_specs=[vmem] * 3,
-        scratch_shapes=[pltpu.VMEM((SIDES_PAD, PTS), F32)],
+        scratch_shapes=[pltpu.VMEM((SIDES_PAD, PTS), F32), pltpu.VMEM((SIDES_PAD, LANES), F32)],
         name="solve",
     )(image, total, solution, residual, direction)
 

time: 84.6 us -> 81.5 us (0.963)
  Pallas kernels: 81.7 us -> 80 us
  local copies, waits for them, and re-layouts: 1.35 us -> 0 us
    pallas_call x1, Pallas kernels: 78.1 us -> 76.3 us  [on_device(): pl.pallas_call(kernel, out_shape=[jax.ShapeDtypeStruct((SIDES_PAD, PTS),...]
where the time goes in v5:
time: 81.5 us; the launch traced here: 81.3 us
  Pallas kernels  80 us (98%)
  between operations  1.28 us (2%)
    pallas_call x1, Pallas kernels, on_device(): pl.pallas_call(kernel, out_shape=[jax.ShapeDtypeStruct((SIDES_PAD, PTS),...  76.3 us
    pallas_call x1, Pallas kernels, on_device(): pl.pallas_call(solve_kernel, out_shape=[jax.ShapeDtypeStruct((SIDES, PTS)...  3.68 us

profile of v5, /device:TPU:1, one launch (start us, length us, event | category | flops | bytes accessed | tf_op | source)
XLA Modules:
  0.0 81.3 jit_solution(1933568625989268243)
XLA Ops:
  1.3 76.3 %block_cg.1 = (f32[24,512]{1,0:T(8,128)}, f32[24,128]{1,0:T(8,128)}) custom-call(f32[32,512]{1,0:T(8,128)} %points.1, f32[1,32]{1,0:T(1,128)} %bitcast.3, f32[1,1]{1,0:T(1,128)} %bitcast.2.noise, f32[17,512]{1,0:T(8,128)} %residual.3, f32[17,512]{1,0:T(8,128)} %direction.3), custom_call_target="tpu_custom_call" | custom-call | flops 30000001024 | bytes 1000000 | tf_op jit(solution)/shard_map/block_cg/pallas_call | solution.py:397
  77.6 3.7 %solve.1 = (f32[17,512]{1,0:T(8,128)}, f32[17,512]{1,0:T(8,128)}, f32[17,512]{1,0:T(8,128)}) custom-call(f32[24,512]{1,0:T(8,128)} %get-tuple-element.5.img24, f32[24,128]{1,0:T(8,128)} %get-tuple-element.6.total_in, f32[17,512]{1,0:T(8,128)} %solution.1, f32[17,512]{1,0:T(8,128)} %residual.3, f32[17,512]{1,0:T(8,128)} %direction.3), custom_call_target="tpu_custom_call" | custom-call | tf_op jit(solution)/shard_map/solve/pallas_call | solution.py:438

commit v6 on v5

--- a/solution.py
+++ b/solution.py
@@ -162,7 +162,7 @@
     middle = ROWS // 2
     for j in range(1, middle):
         gather_copy(j).start()
-    for k in range(1, COLS + 1):
+    for k in range(1, 3):
         column_copy(k).start()
 
     def padded_sides(packet):
@@ -238,6 +238,8 @@
         gather_copy(j).wait_recv()
         load_left(j, gat.at[j])
 
+    for k in range(3, COLS + 1):
+        column_copy(k).start()
     scale_left(0, pl.ds(0, middle * PTS))
     upper_x = jnp.where(x >= SIDE // 2, 2 * PTS, 0)
     upper_z = jnp.where(z >= SIDE // 2, 2 * PTS, 0)
@@ -382,12 +384,13 @@
     inverse = pltpu.roll(work, 96, 1)[:, 0:SIDES_PAD]
 
     step_t = exact_dot(dir_res, inverse)
-    conj_t = exact_dot(exact_dot(step_t, outer) - img_res, inverse)
+    reach = exact_dot(inverse, dirs)
+    conj_left = exact_dot(step_t, outer) - img_res
     moved = exact_dot(step_t, img)
-    new_solution[...] = solution[...] + exact_dot(step_t, dirs)[0:SIDES, :]
+    new_solution[...] = solution[...] + exact_dot(dir_res, reach)[0:SIDES, :]
     res_new = residual[...] - moved[0:SIDES, :]
     new_residual[...] = res_new
-    new_direction[...] = res_new + exact_dot(conj_t, dirs)[0:SIDES, :]
+    new_direction[...] = res_new + exact_dot(conj_left, reach)[0:SIDES, :]
 
 
 def on_device(points, lengthscale, noise, solution, residual, direction):

time: 81.5 us -> 80.1 us (0.983)
  Pallas kernels: 80 us -> 78.6 us
    pallas_call x1, Pallas kernels: 76.3 us -> 75 us  [on_device(): pl.pallas_call(kernel, out_shape=[jax.ShapeDtypeStruct((SIDES_PAD, PTS),...]
where the time goes in v6:
time: 80.1 us; the launch traced here: 79.9 us
  Pallas kernels  78.6 us (98%)
  between operations  1.28 us (2%)
    pallas_call x1, Pallas kernels, on_device(): pl.pallas_call(kernel, out_shape=[jax.ShapeDtypeStruct((SIDES_PAD, PTS),...  75 us
    pallas_call x1, Pallas kernels, on_device(): pl.pallas_call(solve_kernel, out_shape=[jax.ShapeDtypeStruct((SIDES, PTS)...  3.55 us

profile of v6, /device:TPU:1, one launch (start us, length us, event | category | flops | bytes accessed | tf_op | source)
XLA Modules:
  0.0 79.9 jit_solution(17746373687226483202)
XLA Ops:
  1.3 75.0 %block_cg.1 = (f32[24,512]{1,0:T(8,128)}, f32[24,128]{1,0:T(8,128)}) custom-call(f32[32,512]{1,0:T(8,128)} %points.1, f32[1,32]{1,0:T(1,128)} %bitcast.3, f32[1,1]{1,0:T(1,128)} %bitcast.2.noise, f32[17,512]{1,0:T(8,128)} %residual.3, f32[17,512]{1,0:T(8,128)} %direction.3), custom_call_target="tpu_custom_call" | custom-call | flops 30000001024 | bytes 1000000 | tf_op jit(solution)/shard_map/block_cg/pallas_call | solution.py:400
  76.3 3.6 %solve.1 = (f32[17,512]{1,0:T(8,128)}, f32[17,512]{1,0:T(8,128)}, f32[17,512]{1,0:T(8,128)}) custom-call(f32[24,512]{1,0:T(8,128)} %get-tuple-element.5.img24, f32[24,128]{1,0:T(8,128)} %get-tuple-element.6.total_in, f32[17,512]{1,0:T(8,128)} %solution.1, f32[17,512]{1,0:T(8,128)} %residual.3, f32[17,512]{1,0:T(8,128)} %direction.3), custom_call_target="tpu_custom_call" | custom-call | tf_op jit(solution)/shard_map/solve/pallas_call | solution.py:441

commit v7 on v6

--- a/solution.py
+++ b/solution.py
@@ -99,7 +99,7 @@
 
 def kernel(points, lengthscale, noise, residual, direction, img24, total_out,
            pkt, gat, cols, left, ldir, ldirf, ldir8, lscale, right, rdir, rdir8, rscale, side24, fwds, back, rsend, rrecv, bsend, brecv, dir24, res24,
-           gram, ar1, ar2, own,
+           gram, ar1, ar2, own, early,
            gat_send, gat_recv, col_send, col_recv, r_send, r_recv, b_send, b_recv,
            ar1_send, ar1_recv, ar2_send, ar2_recv):
     b = lax.axis_index("blk")
@@ -228,6 +228,8 @@
                 fwds[k, 0:SIDES_PAD] += (low[0:SIDES_PAD] + low[SIDES_PAD:2 * SIDES_PAD]) * lscale[half, :, 0:1]
             waiting = fresh
 
+    other = jnp.concatenate([jnp.zeros((96, PTS), F32), dir24[...], jnp.zeros((8, PTS), F32)], 0)
+    early[...] = exact_dot(res24[...], other, ((1,), (1,)))
     back[...] = jnp.zeros_like(back)
     fwds[...] = jnp.zeros_like(fwds)
     right[0] = expand(pkt[0:FEATS, :], False).astype(BF16)
@@ -311,12 +313,12 @@
         own[0:SIDES, :] += brecv[j]
     img24[...] = own[...] * (LN2 * LN2 / 3.0 / 2.0**BOOST) + noise[...] * dir24[...]
 
-    zeros8 = jnp.zeros((8, PTS), F32)
-    zeros64 = jnp.zeros((64, PTS), F32)
-    img, dirs, res = img24[...], dir24[...], res24[...]
-    table = jnp.concatenate([dirs, zeros8, img, zeros8, zeros64], 0)
-    other = jnp.concatenate([zeros64, img, zeros8, dirs, zeros8], 0)
-    gram[...] = (exact_dot(img, table, ((1,), (1,))) + exact_dot(res, other, ((1,), (1,))))[0:SIDES, :]
+    img = img24[...]
+    table = jnp.concatenate([img, jnp.zeros((LANES - SIDES_PAD, PTS), F32)], 0)
+    products = exact_dot(jnp.concatenate([dir24[...], img, res24[...]], 0), table, ((1,), (1,)))
+    near = pltpu.roll(products[SIDES_PAD:2 * SIDES_PAD], 32, 1)
+    far = pltpu.roll(products[2 * SIDES_PAD:3 * SIDES_PAD], 64, 1)
+    gram[...] = (products[0:SIDES_PAD] + near + far + early[...])[0:SIDES, :]
 
     def ar1_copy(j):
         return pltpu.make_async_remote_copy(
@@ -428,6 +430,7 @@
             pltpu.VMEM((ROWS, SIDES, LANES), F32),
             pltpu.VMEM((PLANE, SIDES, LANES), F32),
             pltpu.VMEM((SIDES_PAD, PTS), F32),
+            pltpu.VMEM((SIDES_PAD, LANES), F32),
             sem((ROWS,)), sem((ROWS,)), sem((COLS + 1,)), sem((COLS + 1,)),
             sem((COLS + 1,)), sem((COLS + 1,)), sem((ROWS,)), sem((ROWS,)),
             sem((ROWS,)), sem((ROWS,)), sem((PLANE,)), sem((PLANE,)),

time: 80.1 us -> 80.1 us (level)
  no operation moved by 1% of the time
where the time goes in v7:
time: 80.1 us; the launch traced here: 79.8 us
  Pallas kernels  78.5 us (98%)
  between operations  1.28 us (2%)
    pallas_call x1, Pallas kernels, on_device(): pl.pallas_call(kernel, out_shape=[jax.ShapeDtypeStruct((SIDES_PAD, PTS),...  75 us
    pallas_call x1, Pallas kernels, on_device(): pl.pallas_call(solve_kernel, out_shape=[jax.ShapeDtypeStruct((SIDES, PTS)...  3.55 us

profile of v7, /device:TPU:1, one launch (start us, length us, event | category | flops | bytes accessed | tf_op | source)
XLA Modules:
  0.0 79.8 jit_solution(10990341415874916610)
XLA Ops:
  1.3 75.0 %block_cg.1 = (f32[24,512]{1,0:T(8,128)}, f32[24,128]{1,0:T(8,128)}) custom-call(f32[32,512]{1,0:T(8,128)} %points.1, f32[1,32]{1,0:T(1,128)} %bitcast.3, f32[1,1]{1,0:T(1,128)} %bitcast.2.noise, f32[17,512]{1,0:T(8,128)} %residual.3, f32[17,512]{1,0:T(8,128)} %direction.3), custom_call_target="tpu_custom_call" | custom-call | flops 30000001024 | bytes 1000000 | tf_op jit(solution)/shard_map/block_cg/pallas_call | solution.py:402
  76.3 3.6 %solve.1 = (f32[17,512]{1,0:T(8,128)}, f32[17,512]{1,0:T(8,128)}, f32[17,512]{1,0:T(8,128)}) custom-call(f32[24,512]{1,0:T(8,128)} %get-tuple-element.5.img24, f32[24,128]{1,0:T(8,128)} %get-tuple-element.6.total_in, f32[17,512]{1,0:T(8,128)} %solution.1, f32[17,512]{1,0:T(8,128)} %residual.3, f32[17,512]{1,0:T(8,128)} %direction.3), custom_call_target="tpu_custom_call" | custom-call | tf_op jit(solution)/shard_map/solve/pallas_call | solution.py:444
